TPU v7x, 128 devices: a whole 4x4x4 slice. The times are simulated.
128 devices in a mesh: dp: 8 (over y, core), ctx: 16 (over x, z).
Axes of the slice: x: 4, y: 4, z: 4, core: 2. Of those that a mesh axis runs over, the one named last changes fastest.
Arguments:
- queries: bfloat16 [8, 4096, 4096], P('dp', 'ctx'), may hold values from -6 to 6
- keys_in: bfloat16 [8, 4096, 4096], P('dp', 'ctx'), may hold values from -6 to 6
- values_in: bfloat16 [8, 4096, 4096], P('dp', 'ctx'), may hold values from -6 to 6
- filters: float32 [4096, 4096], P('ctx'), may hold values from -0.09375 to 0.09375
- skip_gain: float32 [4096], replicated, may hold values from -4 to 4
- out_weight: bfloat16 [4096, 4096], P(None, ('dp', 'ctx')), may hold values from -0.09375 to 0.09375
Outputs:
- projected: bfloat16 [8, 4096, 4096], P('dp', 'ctx')
All inputs are finite; a program needn't handle non-finite values.
Results may differ from a plain program's by a relative error of at most 0.0064.
Values may be sent and summed in bfloat16 or wider, within the bound.
No kernel may reach another device: no remote copies, remote signals or barrier semaphores. Data moves between devices by JAX's collectives and lax.ppermute only.
A program may use at most 256 MiB of HBM per device.

v0:
```python
import math

import jax
import jax.numpy as jnp
from jax import lax
from jax.sharding import PartitionSpec as P


def angles(count_rows, count_cols, period):
    index = (
        jnp.arange(count_rows, dtype=jnp.int32)[:, None]
        * jnp.arange(count_cols, dtype=jnp.int32)[None, :]
        % period
    )
    theta = index.astype(jnp.float32) * (2.0 * math.pi / period)
    return (jnp.cos(theta), jnp.sin(theta))


def close_einsum(form, left, right):
    return jnp.einsum(form, left, right, precision=lax.Precision.HIGH)


def split_einsum(form, table, signal):
    table_high = lax.optimization_barrier(table.astype(jnp.bfloat16))
    table_low = (table - table_high.astype(jnp.float32)).astype(jnp.bfloat16)
    first_part = jnp.einsum(form, table_high, signal, preferred_element_type=jnp.float32)
    return first_part + jnp.einsum(form, table_low, signal, preferred_element_type=jnp.float32)


def forward(signal):
    half = signal.shape[1]
    full = 2 * half
    outer_cos, outer_sin = angles(full, half, full)
    twist_cos, twist_sin = angles(full, 128, full * 128)
    inner_cos, inner_sin = angles(128, 128, 128)
    twist_cos = twist_cos[:, :, None]
    twist_sin = twist_sin[:, :, None]
    if signal.dtype == jnp.bfloat16:
        first_re = split_einsum("kn,snbc->skbc", outer_cos, signal)
        first_im = -split_einsum("kn,snbc->skbc", outer_sin, signal)
    else:
        first_re = close_einsum("kn,snbc->skbc", outer_cos, signal)
        first_im = -close_einsum("kn,snbc->skbc", outer_sin, signal)
    middle_re = first_re * twist_cos + first_im * twist_sin
    middle_im = first_im * twist_cos - first_re * twist_sin
    spec_re = close_einsum("hb,skbc->skhc", inner_cos, middle_re) + close_einsum(
        "hb,skbc->skhc", inner_sin, middle_im
    )
    spec_im = close_einsum("hb,skbc->skhc", inner_cos, middle_im) - close_einsum(
        "hb,skbc->skhc", inner_sin, middle_re
    )
    return (spec_re, spec_im)


def inverse(spec_re, spec_im):
    full = spec_re.shape[1]
    half = full // 2
    outer_cos, outer_sin = angles(full, half, full)
    twist_cos, twist_sin = angles(full, 128, full * 128)
    inner_cos, inner_sin = angles(128, 128, 128)
    twist_cos = twist_cos[:, :, None]
    twist_sin = twist_sin[:, :, None]
    back_re = close_einsum("hb,skhc->skbc", inner_cos, spec_re) - close_einsum(
        "hb,skhc->skbc", inner_sin, spec_im
    )
    back_im = close_einsum("hb,skhc->skbc", inner_cos, spec_im) + close_einsum(
        "hb,skhc->skbc", inner_sin, spec_re
    )
    turned_re = back_re * twist_cos - back_im * twist_sin
    turned_im = back_im * twist_cos + back_re * twist_sin
    result = close_einsum("kn,skbc->snbc", outer_cos, turned_re) - close_einsum(
        "kn,skbc->snbc", outer_sin, turned_im
    )
    return result * (1.0 / (full * 128))


def on_device(queries, keys_in, values_in, filters, skip_gain, out_weight):
    product = (keys_in.astype(jnp.float32) * values_in.astype(jnp.float32)).astype(jnp.bfloat16)
    channels = filters.shape[0]
    length = filters.shape[1]
    half = length // 128
    response = filters.T.reshape(1, half, 128, channels)
    filt_re, filt_im = forward(response)
    local_skip = lax.dynamic_slice_in_dim(skip_gain, lax.axis_index("ctx") * channels, channels)
    piece = lax.all_to_all(product, "ctx", split_axis=2, concat_axis=1, tiled=True)
    count = piece.shape[0]
    signal = piece.astype(jnp.float32)
    spec_re, spec_im = forward(piece.reshape(count, half, 128, channels))
    prod_re = spec_re * filt_re - spec_im * filt_im
    prod_im = spec_re * filt_im + spec_im * filt_re
    causal = inverse(prod_re, prod_im).reshape(count, length, channels)
    mixed = (causal + local_skip[None, None, :] * signal).astype(jnp.bfloat16)
    returned = lax.all_to_all(mixed, "ctx", split_axis=1, concat_axis=2, tiled=True)
    gated = (queries.astype(jnp.float32) * returned.astype(jnp.float32)).astype(jnp.bfloat16)
    seq_count, tok_count, width = gated.shape
    tok_rows = gated.reshape(seq_count * tok_count, width)
    result = jnp.dot(
        tok_rows,
        lax.all_gather(out_weight, ("dp", "ctx"), axis=1, tiled=True),
        preferred_element_type=jnp.float32,
    ).astype(jnp.bfloat16)
    return result.reshape(seq_count, tok_count, result.shape[1])


def solution(mesh):
    in_specs = (
        P("dp", "ctx", None),
        P("dp", "ctx", None),
        P("dp", "ctx", None),
        P("ctx", None),
        P(),
        P(None, ("dp", "ctx")),
    )
    out_specs = P("dp", "ctx", None)
    return jax.shard_map(
        on_device, mesh=mesh, in_specs=in_specs, out_specs=out_specs, check_vma=False
    )
```

profile of v0, /device:TPU:1, one launch (start us, length us, event | category | flops | bytes accessed | tf_op | source)
XLA Modules:
  0.0 451.7 jit_solution(194958502813728175)
XLA Ops:
  10.3 7.3 %copy.93 = bf16[1,256,4096]{1,0,2:T(2,128)(2,1)} copy(bf16[1,256,4096]{2,1,0:T(8,128)(2,1)S(1)} %multiply_convert_fusion) | data formatting | bytes 4194304 | tf_op jit(solution)/shard_map/convert_element_type | solution.py:78
  18.1 21.6 %reduce = bf16[4096,256]{1,0:T(8,128)(2,1)S(1)} reduce(bf16[4096,1,256]{2,1,0:T(2,128)(2,1)} %bitcast.223, bf16[]{:T(256)} %broadcast.280), dimensions={1}, to_apply=%bitcast.182.reduce_sub_computation | reduce | bytes 4194306
  41.7 8.6 %all-to-all-start = ((bf16[16,2,32768]{2,1,0:T(2,128)(2,1)}), bf16[16,2,32768]{2,1,0:T(2,128)(2,1)S(1)}, u32[]{:S(2)}, u32[]{:S(2)}) async-start(bf16[16,2,32768]{2,1,0:T(2,128)(2,1)} %reshape.237), calls=%async_computation | async-start | bytes 4194304 | tf_op jit(solution)/shard_map/all_to_all | solution.py:85
  63.1 9.0 %fusion.82 = f32[64,128,256]{2,0,1:T(8,128)} fusion(f32[32,128,256]{2,0,1:T(8,128)} %copy.103), kind=kOutput, calls=%fused_computation.100 | convolution fusion | flops 402681856 | bytes 12582912 | tf_op jit(solution)/shard_map/kn,snbc->skbc/dot_general | solution.py:20
  78.1 8.7 %all-to-all-done = bf16[16,2,32768]{2,1,0:T(2,128)(2,1)S(1)} async-done(((bf16[16,2,32768]{2,1,0:T(2,128)(2,1)}), bf16[16,2,32768]{2,1,0:T(2,128)(2,1)S(1)}, u32[]{:S(2)}, u32[]{:S(2)}) %all-to-all-start) | async-done | bytes 2097184 | tf_op jit(solution)/shard_map/all_to_all | solution.py:85
  86.8 6.8 %reshape.238 = bf16[4096,1,256]{2,1,0:T(2,128)(2,1)} reshape(bf16[16,2,32768]{2,1,0:T(2,128)(2,1)S(1)} %all-to-all-done) | data formatting | bytes 4194304
  117.3 23.7 %fusion.17 = (f32[64,128,256]{2,0,1:T(8,128)}, f32[64,128,256]{2,0,1:T(8,128)}, f32[64,128,256]{2,0,1:T(8,128)}, f32[64,128,256]{2,0,1:T(8,128)}) fusion(f32[128,256,64]{1,2,0:T(8,128)} %add_negate_fusion, f32[64,128]{0,1:T(8,128)S(1)} %copy.100, f32[64,128]{0,1:T(8,128)S(1)} %copy.97, f32[128,256,64]{1,2,0:T(8,128)} %fusion.28, ...), kind=kOutput, calls=%fused_computation.27 | convolution fusion | flops 163577856 | bytes 69275648 | tf_op jit(solution)/shard_map/kn,snbc->skbc/dot_general | solution.py:26
  141.0 9.3 %copy.105 = f32[64,128,256]{1,2,0:T(8,128)} copy(f32[64,128,256]{2,0,1:T(8,128)} %get-tuple-element.14) | data formatting | bytes 16777216 | tf_op jit(solution)/shard_map/reshape.26
  150.3 9.3 %copy.101 = f32[64,128,256]{1,2,0:T(8,128)} copy(f32[64,128,256]{2,0,1:T(8,128)} %get-tuple-element.9) | data formatting | bytes 16777216 | tf_op jit(solution)/shard_map/reshape.16
  159.5 9.3 %copy.106 = f32[64,128,256]{1,2,0:T(8,128)} copy(f32[64,128,256]{2,0,1:T(8,128)} %get-tuple-element.13) | data formatting | bytes 16777216 | tf_op jit(solution)/shard_map/reshape.28
  168.8 9.3 %copy.102 = f32[64,128,256]{1,2,0:T(8,128)} copy(f32[64,128,256]{2,0,1:T(8,128)} %get-tuple-element.10) | data formatting | bytes 16777216 | tf_op jit(solution)/shard_map/reshape.20
  178.1 8.7 %fusion.43 = f32[64,256,128]{2,1,0:T(8,128)} fusion(f32[64,128,256]{1,2,0:T(8,128)} %copy.102), kind=kOutput, calls=%fused_computation.67 | convolution fusion | flops 1610842112 | bytes 16777216 | tf_op jit(solution)/shard_map/hb,skbc->skhc/dot_general | solution.py:20
  186.7 6.6 %fusion.49 = f32[64,256,128]{2,1,0:T(8,128)} fusion(f32[64,128,256]{1,2,0:T(8,128)S(1)} %copy-done.1), kind=kOutput, calls=%fused_computation.73 | convolution fusion | flops 1610842112 | bytes 16777216 | tf_op jit(solution)/shard_map/hb,skbc->skhc/dot_general | solution.py:20
  224.2 29.1 %multiply_subtract_fusion = (f32[64,256,128]{2,1,0:T(8,128)}, f32[64,256,128]{2,1,0:T(8,128)}) fusion(f32[64,256,128]{2,1,0:T(8,128)} %fusion.37, f32[64,256,128]{2,1,0:T(8,128)} %fusion.49, f32[64,256,128]{2,1,0:T(8,128)} %fusion.39, f32[64,256,128]{2,1,0:T(8,128)} %fusion.51, f32[64,256,128]{2,1,0:T(8,128)} %fusion.41, f32[64,256,128]{2,1,0:T(8,128)} %fusion.53, ...), kind=kOutput, calls=%fused_computation.33 | convolution fusion | flops 1631813632 | bytes 83886080 | tf_op jit(solution)/shard_map/hb,skbc->skhc/dot_general | solution.py:20
  253.3 8.7 %fusion.4 = f32[64,256,128]{2,1,0:T(8,128)} fusion(f32[64,256,128]{2,1,0:T(8,128)} %get-tuple-element.5), kind=kOutput, calls=%fused_computation.6 | convolution fusion | flops 1610842112 | bytes 16777216 | tf_op jit(solution)/shard_map/hb,skhc->skbc/dot_general | solution.py:20
  274.1 19.6 %fusion.3 = (f32[64,128,256]{1,2,0:T(8,128)}, f32[64,128,256]{1,2,0:T(8,128)}) fusion(f32[64,128]{1,0:T(8,128)S(1)} %get-tuple-element.15, f32[64,128]{1,0:T(8,128)S(1)} %get-tuple-element.16, f32[64,256,128]{2,1,0:T(8,128)} %fusion.8, f32[64,256,128]{2,1,0:T(8,128)} %fusion.4, f32[64,256,128]{2,1,0:T(8,128)} %fusion.6, f32[64,256,128]{2,1,0:T(8,128)} %get-tuple-element.6), kind=kOutput, calls=%fused_computation.5 | convolution fusion | flops 1627619328 | bytes 50397184 | tf_op jit(solution)/shard_map/hb,skhc->skbc/dot_general | solution.py:20
  293.7 9.2 %copy.111 = f32[64,128,256]{2,0,1:T(8,128)} copy(f32[64,128,256]{1,2,0:T(8,128)} %get-tuple-element.8) | data formatting | bytes 16777216 | tf_op jit(solution)/shard_map/reshape.46
  302.9 9.2 %copy.112 = f32[64,128,256]{2,0,1:T(8,128)} copy(f32[64,128,256]{1,2,0:T(8,128)} %get-tuple-element.7) | data formatting | bytes 16777216 | tf_op jit(solution)/shard_map/reshape.48
  324.6 25.3 %copy.131 = bf16[1,4096,256]{2,0,1:T(2,128)(2,1)} copy(bf16[1,4096,256]{2,1,0:T(8,128)(2,1)S(1)} %fusion.23) | data formatting | bytes 4194304 | tf_op jit(solution)/shard_map/convert_element_type | solution.py:92
  349.9 21.6 %reduce.1 = bf16[4096,256]{1,0:T(8,128)(2,1)S(1)} reduce(bf16[4096,1,256]{2,1,0:T(2,128)(2,1)} %bitcast.224, bf16[]{:T(256)} %broadcast.280), dimensions={1}, to_apply=%bitcast.208.reduce_sub_computation | reduce | bytes 4194306
  373.5 6.4 %all-to-all-start.1 = ((bf16[16,2,32768]{2,1,0:T(2,128)(2,1)}), bf16[16,2,32768]{2,1,0:T(2,128)(2,1)S(1)}, u32[]{:S(2)}, u32[]{:S(2)}) async-start(bf16[16,2,32768]{2,1,0:T(2,128)(2,1)} %reshape.239), calls=%async_computation.1 | async-start | bytes 4194304 | tf_op jit(solution)/shard_map/all_to_all | solution.py:93
  384.0 22.3 %all-to-all-done.1 = bf16[16,2,32768]{2,1,0:T(2,128)(2,1)S(1)} async-done(((bf16[16,2,32768]{2,1,0:T(2,128)(2,1)}), bf16[16,2,32768]{2,1,0:T(2,128)(2,1)S(1)}, u32[]{:S(2)}, u32[]{:S(2)}) %all-to-all-start.1) | async-done | bytes 2097184 | tf_op jit(solution)/shard_map/all_to_all | solution.py:93
  406.4 6.8 %reshape.240 = bf16[4096,1,256]{2,1,0:T(2,128)(2,1)} reshape(bf16[16,2,32768]{2,1,0:T(2,128)(2,1)S(1)} %all-to-all-done.1) | data formatting | bytes 4194304
  427.5 16.9 %fusion.20 = bf16[1,256,4096]{2,1,0:T(8,128)(2,1)} fusion(bf16[4096,4096]{0,1:T(8,128)(2,1)} %all-gather.2.cloned.1.call-done, bf16[1,256,4096]{1,2,0:T(8,128)(2,1)} %fusion.21), kind=kOutput, calls=%fused_computation.36 | convolution fusion | flops 8590983168 | bytes 37748736 | tf_op jit(solution)/shard_map/dot_general | solution.py:97
  (72 shorter events, 124.6 us)
Async XLA Ops:
  6.5 421.0 %all-gather.2.cloned.1.call-start = ((), (), s32[]{:S(2)}) async-start(), calls=%async_computation.2 | async-start | bytes 33816576 | tf_op jit(solution)/shard_map/all_gather | solution.py:99
  41.7 45.1 %all-to-all-start = ((bf16[16,2,32768]{2,1,0:T(2,128)(2,1)}), bf16[16,2,32768]{2,1,0:T(2,128)(2,1)S(1)}, u32[]{:S(2)}, u32[]{:S(2)}) async-start(bf16[16,2,32768]{2,1,0:T(2,128)(2,1)} %reshape.237), calls=%async_computation | async-start | bytes 4194304 | tf_op jit(solution)/shard_map/all_to_all | solution.py:85
  61.6 10.4 %copy-start.2 = (f32[32,128,256]{2,0,1:T(8,128)S(1)}, f32[32,128,256]{2,0,1:T(8,128)}, u32[]{:S(2)}) copy-start(f32[32,128,256]{2,0,1:T(8,128)} %copy.103) | copy-start | bytes 12582916
  178.1 8.7 %copy-start.1 = (f32[64,128,256]{1,2,0:T(8,128)S(1)}, f32[64,128,256]{1,2,0:T(8,128)}, u32[]{:S(2)}) copy-start(f32[64,128,256]{1,2,0:T(8,128)} %copy.102) | copy-start | bytes 25165828
  178.1 15.2 %slice-start.6 = ((s8[8388608]{0:T(1024)(128)(4,1)}), s8[4194304]{0:T(1024)(128)(4,1)S(1)}, s32[]{:S(2)}) async-start(s8[8388608]{0:T(1024)(128)(4,1)} %bitcast.215), calls=%async_computation.9 | async-start | bytes 8388608
  186.7 6.6 %slice-start.7 = ((s8[8388608]{0:T(1024)(128)(4,1)}), s8[4194304]{0:T(1024)(128)(4,1)S(1)}, s32[]{:S(2)}) async-start(s8[8388608]{0:T(1024)(128)(4,1)} %bitcast.215), calls=%async_computation.10 | async-start | bytes 8388608
  193.3 12.3 %slice-start.4 = ((s8[8388608]{0:T(1024)(128)(4,1)}), s8[4194304]{0:T(1024)(128)(4,1)S(1)}, s32[]{:S(2)}) async-start(s8[8388608]{0:T(1024)(128)(4,1)} %bitcast.213), calls=%async_computation.7 | async-start | bytes 8388608
  199.5 6.1 %slice-start.5 = ((s8[8388608]{0:T(1024)(128)(4,1)}), s8[4194304]{0:T(1024)(128)(4,1)S(1)}, s32[]{:S(2)}) async-start(s8[8388608]{0:T(1024)(128)(4,1)} %bitcast.213), calls=%async_computation.8 | async-start | bytes 8388608
  205.6 12.2 %slice-start = ((s8[8388608]{0:T(1024)(128)(4,1)}), s8[4194304]{0:T(1024)(128)(4,1)S(1)}, s32[]{:S(2)}) async-start(s8[8388608]{0:T(1024)(128)(4,1)} %bitcast.209), calls=%async_computation.3 | async-start | bytes 8388608
  211.7 6.1 %slice-start.1 = ((s8[8388608]{0:T(1024)(128)(4,1)}), s8[4194304]{0:T(1024)(128)(4,1)S(1)}, s32[]{:S(2)}) async-start(s8[8388608]{0:T(1024)(128)(4,1)} %bitcast.209), calls=%async_computation.4 | async-start | bytes 8388608
  253.2 8.7 %copy-start = (f32[64,256,128]{2,1,0:T(8,128)S(1)}, f32[64,256,128]{2,1,0:T(8,128)}, u32[]{:S(2)}) copy-start(f32[64,256,128]{2,1,0:T(8,128)} %get-tuple-element.5) | copy-start | bytes 25165828
  253.2 14.8 %slice-start.2 = ((s8[8388608]{0:T(1024)(128)(4,1)}), s8[4194304]{0:T(1024)(128)(4,1)S(1)}, s32[]{:S(2)}) async-start(s8[8388608]{0:T(1024)(128)(4,1)} %bitcast.211), calls=%async_computation.5 | async-start | bytes 8388608
  261.9 6.1 %slice-start.3 = ((s8[8388608]{0:T(1024)(128)(4,1)}), s8[4194304]{0:T(1024)(128)(4,1)S(1)}, s32[]{:S(2)}) async-start(s8[8388608]{0:T(1024)(128)(4,1)} %bitcast.211), calls=%async_computation.6 | async-start | bytes 8388608
  312.1 5.8 %copy-start.3 = (f32[64,128,256]{2,0,1:T(8,128)S(1)}, f32[64,128,256]{2,0,1:T(8,128)}, u32[]{:S(2)}) copy-start(f32[64,128,256]{2,0,1:T(8,128)} %copy.112) | copy-start | bytes 25165828
  321.0 2.5 copy-start.4
  321.0 2.5 copy-start.6
  373.5 32.9 %all-to-all-start.1 = ((bf16[16,2,32768]{2,1,0:T(2,128)(2,1)}), bf16[16,2,32768]{2,1,0:T(2,128)(2,1)S(1)}, u32[]{:S(2)}, u32[]{:S(2)}) async-start(bf16[16,2,32768]{2,1,0:T(2,128)(2,1)} %reshape.239), calls=%async_computation.1 | async-start | bytes 4194304 | tf_op jit(solution)/shard_map/all_to_all | solution.py:93
  415.7 7.8 %copy-start.5 = (bf16[1,256,4096]{1,2,0:T(8,128)(2,1)S(1)}, bf16[1,256,4096]{1,2,0:T(8,128)(2,1)}, u32[]{:S(2)}) copy-start(bf16[1,256,4096]{1,2,0:T(8,128)(2,1)} %copy.92) | copy-start | bytes 6291460
Sparse Core Ops, SparseCore 0:
  10.5 130.8 all-gather.1
where the time goes:
time: 460 us; the launch traced here: 452 us
  matrix products  192 us (42%)
  local copies, waits for them, and re-layouts  145 us (32%)
  other arithmetic  54 us (12%)
  waiting for transfers between devices  31.8 us (7%)
  starting transfers between devices  15.1 us (3%)
  between operations  14 us (3%)
    dot_general x16, matrix products, close_einsum(): return jnp.einsum(form, left, right, precision=lax.Precision.HIGH)  138 us
    another operation x7, local copies, waits for them, and re-layouts  61.1 us
    unnamed x6, other arithmetic  43.1 us
    unnamed x38, local copies, waits for them, and re-layouts  32.1 us
    convert_element_type x1, local copies, waits for them, and re-layouts, on_device(): mixed = (causal + local_skip[None, None, :] * signal).astype(jnp.bfloat16)  25.3 us
    dot_general x2, matrix products, split_einsum(): jnp.einsum(form, table_high, signal, preferred_element_type=jnp.float32)  25.2 us
    all_to_all x1, waiting for transfers between devices, on_device(): lax.all_to_all(mixed, 'ctx', split_axis=1, concat_axis=2, tiled=True)  22.3 us
    dot_general x1, matrix products, on_device(): jnp.dot(tok_rows, lax.all_gather(out_weight, ('dp', 'ctx'), axis=1, tiled...  16.9 us
  transfers between devices with their start and end apart: 3, of which 2 were waited for; matrix products, arithmetic and copies ran while one was open for 83% of the time, Pallas kernels for 0%

commit v1 on v0

v1 whole, which is shorter than its diff:
```python
import math

import jax
import jax.numpy as jnp
import ml_dtypes
import numpy as np
from jax import lax
from jax.experimental import pallas as pl
from jax.experimental.pallas import tpu as pltpu
from jax.sharding import PartitionSpec as P

F32 = jnp.float32
BF16 = jnp.bfloat16
MIB = 1024 * 1024

OUTER = 32
INNER = 128


def split_table(table):
    high = table.astype(ml_dtypes.bfloat16)
    low = (table - high.astype(np.float64)).astype(ml_dtypes.bfloat16)
    return high, low


def tables():
    length = OUTER * INNER
    k1 = np.arange(OUTER)[:, None, None]
    k2 = np.arange(INNER)[None, :, None]
    b = np.arange(INNER)[None, None, :]
    theta = 2.0 * math.pi * b * (k1 + 0.25 + OUTER * k2) / length
    cos, sin = np.cos(theta), np.sin(theta)
    top = np.concatenate([cos, sin], axis=2)
    bottom = np.concatenate([-sin, cos], axis=2)
    forward = np.concatenate([top, bottom], axis=1)
    backward = np.swapaxes(forward, 1, 2) / length
    return split_table(forward) + split_table(backward)


def cadd(u, v):
    return (u[0] + v[0], u[1] + v[1])


def csub(u, v):
    return (u[0] - v[0], u[1] - v[1])


def turn(u, angle):
    quarter = round(angle / (math.pi / 2), 9)
    if quarter == int(quarter):
        quarter = int(quarter) % 4
        if quarter == 0:
            return u
        if quarter == 1:
            return (-u[1], u[0])
        if quarter == 2:
            return (-u[0], -u[1])
        return (u[1], -u[0])
    c, s = math.cos(angle), math.sin(angle)
    return (u[0] * c - u[1] * s, u[0] * s + u[1] * c)


def four(u, sign):
    p, q = cadd(u[0], u[2]), csub(u[0], u[2])
    r, t = cadd(u[1], u[3]), csub(u[1], u[3])
    if sign < 0:
        t = (t[1], -t[0])
    else:
        t = (-t[1], t[0])
    return [cadd(p, r), cadd(q, t), csub(p, r), csub(q, t)]


def eight(u, sign):
    even = four(u[0::2], sign)
    odd = four(u[1::2], sign)
    half = math.sqrt(0.5)
    o1, o3 = odd[1], odd[3]
    if sign < 0:
        odd[1] = ((o1[0] + o1[1]) * half, (o1[1] - o1[0]) * half)
        odd[2] = (odd[2][1], -odd[2][0])
        odd[3] = ((o3[1] - o3[0]) * half, (o3[0] + o3[1]) * -half)
    else:
        odd[1] = ((o1[0] - o1[1]) * half, (o1[0] + o1[1]) * half)
        odd[2] = (-odd[2][1], odd[2][0])
        odd[3] = ((o3[0] + o3[1]) * -half, (o3[0] - o3[1]) * half)
    return [cadd(even[i], odd[i]) for i in range(4)] + [csub(even[i], odd[i]) for i in range(4)]


def outer_forward(x):
    c1, s1 = math.cos(math.pi / 8), math.sin(math.pi / 8)
    half = math.sqrt(0.5)
    rows = []
    for r in range(8):
        x0, x1, x2, x3 = x[r], x[r + 8], x[r + 16], x[r + 24]
        x2 = x2 * half
        y0, y1 = (x0 + x2, -x2), (x0 - x2, x2)
        u1, v1 = x1 * c1, x1 * s1
        u3, v3 = x3 * s1, x3 * c1
        p = (u1 + u3, -(v1 + v3))
        d = (u1 - u3, v3 - v1)
        d = (d[1], -d[0])
        rows.append([cadd(y0, p), cadd(y1, d), csub(y0, p), csub(y1, d)])
    out = [None] * OUTER
    for q in range(4):
        column = [turn(rows[r][q], -2.0 * math.pi * r * (q + 0.25) / OUTER) for r in range(8)]
        for k, value in enumerate(eight(column, -1)):
            out[q + 4 * k] = value
    return out


def outer_backward(t):
    columns = []
    for q in range(4):
        g = eight([t[q + 4 * k] for k in range(8)], 1)
        columns.append([turn(g[r], 2.0 * math.pi * r * (q + 0.25) / OUTER) for r in range(8)])
    out = [None] * OUTER
    for r in range(8):
        v = [columns[q][r] for q in range(4)]
        p, s = cadd(v[0], v[2]), csub(v[0], v[2])
        w, d = cadd(v[1], v[3]), csub(v[1], v[3])
        out[r] = p[0] + w[0]
        for j, (re, im) in (
            (1, (s[0] - d[1], s[1] + d[0])),
            (2, csub(p, w)),
            (3, (s[0] + d[1], s[1] - d[0])),
        ):
            c, n = math.cos(math.pi * j / 8), math.sin(math.pi * j / 8)
            out[r + 8 * j] = re * c - im * n
    return out


def split(value):
    high = value.astype(BF16)
    return high, (value - high.astype(F32)).astype(BF16)


def close_dot(high, low, value):
    value_high, value_low = split(value)
    return (
        jnp.dot(high, value_high, preferred_element_type=F32)
        + jnp.dot(high, value_low, preferred_element_type=F32)
        + jnp.dot(low, value_high, preferred_element_type=F32)
    )


def product_kernel(keys_ref, values_ref, out_ref):
    out_ref[0] = (keys_ref[...].astype(F32) * values_ref[...].astype(F32)).astype(BF16)


def product_blocks(keys, values, parts):
    rows, width = keys.shape
    cols = width // parts
    return pl.pallas_call(
        product_kernel,
        grid=(parts,),
        in_specs=[pl.BlockSpec((rows, cols), lambda j: (0, j))] * 2,
        out_specs=pl.BlockSpec((1, rows, cols), lambda j: (j, 0, 0)),
        out_shape=jax.ShapeDtypeStruct((parts, rows, cols), BF16),
        cost_estimate=pl.CostEstimate(flops=rows * width, bytes_accessed=6 * rows * width, transcendentals=0),
        name="product",
    )(keys, values)


def spectrum_kernel(filters_ref, high_ref, low_ref, out_ref, taps, high, low, sems):
    chunks = 8
    step = OUTER // chunks

    def fetch(i):
        part = pl.ds(i * step, step)
        return (
            pltpu.make_async_copy(high_ref.at[part], high.at[part], sems.at[0, i]),
            pltpu.make_async_copy(low_ref.at[part], low.at[part], sems.at[1, i]),
        )

    for i in range(chunks):
        for copy in fetch(i):
            copy.start()
    for a in range(OUTER):
        taps[pl.ds(a * INNER, INNER), :] = filters_ref[:, pl.ds(a * INNER, INNER)].T

    def outer(i, carry):
        base = pl.multiple_of(i * 8, 8)
        x = [taps[pl.ds(a * INNER + base, 8), :] for a in range(OUTER)]
        for k, (re, im) in enumerate(outer_forward(x)):
            out_ref[k, pl.ds(base, 8), :] = re
            out_ref[k, pl.ds(INNER + base, 8), :] = im
        return carry

    lax.fori_loop(0, INNER // 8, outer, 0)
    for i in range(chunks):
        for copy in fetch(i):
            copy.wait()

        def inner(k, carry):
            out_ref[k] = close_dot(high[k], low[k], out_ref[k])
            return carry

        lax.fori_loop(i * step, (i + 1) * step, inner, 0)


def filter_spectrum(filters, high, low):
    channels, length = filters.shape
    lanes = 128
    size = 2 * INNER
    return pl.pallas_call(
        spectrum_kernel,
        grid=(channels // lanes,),
        in_specs=[
            pl.BlockSpec((lanes, length), lambda j: (j, 0)),
            pl.BlockSpec(memory_space=pl.ANY),
            pl.BlockSpec(memory_space=pl.ANY),
        ],
        out_specs=pl.BlockSpec((OUTER, size, lanes), lambda j: (0, 0, j)),
        out_shape=jax.ShapeDtypeStruct((OUTER, size, channels), F32),
        scratch_shapes=[
            pltpu.VMEM((length, lanes), F32),
            pltpu.VMEM((OUTER, size, size), BF16),
            pltpu.VMEM((OUTER, size, size), BF16),
            pltpu.SemaphoreType.DMA((2, 8)),
        ],
        compiler_params=pltpu.CompilerParams(vmem_limit_bytes=40 * MIB),
        cost_estimate=pl.CostEstimate(
            flops=6 * OUTER * size * size * channels, bytes_accessed=16 * OUTER * size * size, transcendentals=0
        ),
        name="spectrum",
    )(filters, high, low)


def conv_kernel(
    signal_ref, spec_ref, skip_ref, fh_ref, fl_ref, bh_ref, bl_ref, out_ref, work, spec, fh, fl, bh, bl, sems
):
    chunks = 8
    step = OUTER // chunks
    lanes = 128
    channels = out_ref.shape[1]
    pairs = ((fh_ref, fh), (fl_ref, fl), (spec_ref, spec), (bh_ref, bh), (bl_ref, bl))

    def fetch(i):
        part = pl.ds(i * step, step)
        return [
            pltpu.make_async_copy(source.at[part], target.at[part], sems.at[n, i])
            for n, (source, target) in enumerate(pairs)
        ]

    for i in range(chunks):
        for copy in fetch(i):
            copy.start()

    for c in range(0, channels, lanes):
        col = pl.ds(c, lanes)

        def outer(i, carry):
            base = pl.multiple_of(i * 16, 16)
            rows = [signal_ref[pl.ds(a * INNER + base, 16), col].astype(F32) for a in range(OUTER)]
            for h in range(0, 16, 8):
                for k, (re, im) in enumerate(outer_forward([row[h : h + 8] for row in rows])):
                    work[k, pl.ds(base + h, 8), col] = re
                    work[k, pl.ds(INNER + base + h, 8), col] = im
            return carry

        lax.fori_loop(0, INNER // 16, outer, 0)

    for i in range(chunks):
        for copy in fetch(i):
            copy.wait()

        def inner(k, carry):
            value = close_dot(fh[k], fl[k], work[k])
            re, im = value[:INNER], value[INNER:]
            sre, sim = spec[k, :INNER], spec[k, INNER:]
            mixed = jnp.concatenate([re * sre - im * sim, re * sim + im * sre], axis=0)
            work[k] = close_dot(bh[k], bl[k], mixed)
            return carry

        lax.fori_loop(i * step, (i + 1) * step, inner, 0)

    for c in range(0, channels, lanes):
        col = pl.ds(c, lanes)
        gain = skip_ref[:, col]

        def back(i, carry):
            base = pl.multiple_of(i * 16, 16)
            halves = []
            for h in range(0, 16, 8):
                t = [
                    (work[k, pl.ds(base + h, 8), col], work[k, pl.ds(INNER + base + h, 8), col])
                    for k in range(OUTER)
                ]
                halves.append(outer_backward(t))
            for a in range(OUTER):
                rows = pl.ds(a * INNER + base, 16)
                causal = jnp.concatenate([halves[0][a], halves[1][a]], axis=0)
                out_ref[rows, col] = (causal + gain * signal_ref[rows, col].astype(F32)).astype(BF16)
            return carry

        lax.fori_loop(0, INNER // 16, back, 0)


def convolve(signal, spec, skip, table):
    length, channels = signal.shape
    size = 2 * INNER
    anywhere = pl.BlockSpec(memory_space=pl.ANY)
    inside = pl.BlockSpec(memory_space=pltpu.VMEM)
    square = pltpu.VMEM((OUTER, size, size), BF16)
    return pl.pallas_call(
        conv_kernel,
        in_specs=[inside, anywhere, inside] + [anywhere] * 4,
        out_specs=inside,
        out_shape=jax.ShapeDtypeStruct((length, channels), BF16),
        scratch_shapes=[
            pltpu.VMEM((OUTER, size, channels), F32),
            pltpu.VMEM((OUTER, size, channels), F32),
            square,
            square,
            square,
            square,
            pltpu.SemaphoreType.DMA((5, 8)),
        ],
        compiler_params=pltpu.CompilerParams(vmem_limit_bytes=48 * MIB),
        cost_estimate=pl.CostEstimate(
            flops=12 * OUTER * size * size * channels, bytes_accessed=24 * OUTER * size * size, transcendentals=0
        ),
        name="convolve",
    )(signal, spec, skip, *table)


def project_kernel(queries_ref, mixed_ref, weight_ref, out_ref, gated):
    parts = mixed_ref.shape[0]
    width = mixed_ref.shape[2]

    @pl.when(pl.program_id(0) == 0)
    def _():
        for j in range(parts):
            cols = pl.ds(j * width, width)
            gated[:, cols] = (queries_ref[:, cols].astype(F32) * mixed_ref[j].astype(F32)).astype(BF16)

    out_ref[...] = lax.dot_general(
        gated[...], weight_ref[...], (((1,), (1,)), ((), ())), preferred_element_type=F32
    ).astype(BF16)


def project(queries, mixed, weight):
    rows, width = queries.shape
    features = weight.shape[0]
    tile = 512
    return pl.pallas_call(
        project_kernel,
        grid=(features // tile,),
        in_specs=[
            pl.BlockSpec((rows, width), lambda n: (0, 0)),
            pl.BlockSpec(mixed.shape, lambda n: (0, 0, 0)),
            pl.BlockSpec((tile, width), lambda n: (n, 0)),
        ],
        out_specs=pl.BlockSpec((rows, tile), lambda n: (0, n)),
        out_shape=jax.ShapeDtypeStruct((rows, features), BF16),
        scratch_shapes=[pltpu.VMEM((rows, width), BF16)],
        compiler_params=pltpu.CompilerParams(vmem_limit_bytes=40 * MIB),
        cost_estimate=pl.CostEstimate(
            flops=2 * rows * width * features, bytes_accessed=2 * width * features, transcendentals=0
        ),
        name="project",
    )(queries, mixed, weight)


def on_device(queries, keys_in, values_in, filters, skip_gain, out_weight):
    count = lax.axis_size("ctx")
    rows, width = queries.shape[1:]
    cols = width // count
    table = [jnp.asarray(t) for t in tables()]
    weight = lax.all_gather(out_weight.T, ("dp", "ctx"), axis=0, tiled=True)
    product = product_blocks(keys_in[0], values_in[0], count)
    piece = lax.all_to_all(product, "ctx", split_axis=0, concat_axis=0, tiled=True)
    spec = filter_spectrum(filters, table[0], table[1])
    skip = lax.dynamic_slice_in_dim(skip_gain, lax.axis_index("ctx") * cols, cols).reshape(1, cols)
    mixed = convolve(piece.reshape(count * rows, cols), spec, skip, table)
    returned = lax.all_to_all(mixed.reshape(count, rows, cols), "ctx", split_axis=0, concat_axis=0, tiled=True)
    return project(queries[0], returned, weight)[None]


def solution(mesh):
    in_specs = (
        P("dp", "ctx", None),
        P("dp", "ctx", None),
        P("dp", "ctx", None),
        P("ctx", None),
        P(),
        P(None, ("dp", "ctx")),
    )
    return jax.shard_map(
        on_device, mesh=mesh, in_specs=in_specs, out_specs=P("dp", "ctx", None), check_vma=False
    )
```

time: 460 us -> 188 us (0.41); the launches traced: 452 us -> 187 us
  matrix products: 192 us -> 0 us
  local copies, waits for them, and re-layouts: 145 us -> 9 us
  Pallas kernels: 0 us -> 82.1 us
  blocking collectives: 0 us -> 54.3 us
  other arithmetic: 54 us -> 0 us
  waiting for transfers between devices: 31.8 us -> 19.8 us
  starting transfers between devices: 15.1 us -> 8.43 us
    dot_general x21 -> x0, matrix products: 192 us -> none  [the longest x16 138 us: close_einsum(): return jnp.einsum(form, left, right, precision=lax.Precision.HIGH)]
    pallas_call x0 -> x4, Pallas kernels: none -> 82.1 us  [the longest x1 30.5 us: convolve(): pl.pallas_call(conv_kernel, in_specs=[inside, anywhere, inside] + [anywhe...]
    another operation x7 -> x0, local copies, waits for them, and re-layouts: 61.1 us -> none
    all_to_all x0 -> x1, blocking collectives: none -> 54.3 us  [on_device(): lax.all_to_all(mixed.reshape(count, rows, cols), 'ctx', split_axis=0, con...]
    unnamed x6 -> x0, other arithmetic: 43.1 us -> none
    convert_element_type x4 -> x0, local copies, waits for them, and re-layouts: 42.3 us -> none  [the longest x1 25.3 us: on_device(): mixed = (causal + local_skip[None, None, :] * signal).astype(jnp.bfloat16)]
    all_to_all x2 -> x1, waiting for transfers between devices: 31.1 us -> 0.01 us  [on_device(): lax.all_to_all(product, 'ctx', split_axis=0, concat_axis=0, tiled=True)]
    unnamed x38 -> x8, local copies, waits for them, and re-layouts: 32.1 us -> 8.24 us
  transfers between devices with their start and end apart: 3 -> 2, of which waited for: 2 -> 1; matrix products, arithmetic and copies ran while one was open for 83% -> 0% of each run, Pallas kernels for 0% -> 35%
where the time goes in v1:
time: 188 us; the launch traced here: 187 us
  Pallas kernels  82.1 us (44%)
  blocking collectives  54.3 us (29%)
  waiting for transfers between devices  19.8 us (11%)
  between operations  13.4 us (7%)
  local copies, waits for them, and re-layouts  9 us (5%)
  starting transfers between devices  8.43 us (4%)
    all_to_all x1, blocking collectives, on_device(): lax.all_to_all(mixed.reshape(count, rows, cols), 'ctx', split_axis=0, con...  54.3 us
    pallas_call x1, Pallas kernels, convolve(): pl.pallas_call(conv_kernel, in_specs=[inside, anywhere, inside] + [anywhe...  30.5 us
    pallas_call x1, Pallas kernels, filter_spectrum(): pl.pallas_call(spectrum_kernel, grid=(channels // lanes,), in_specs=[pl.B...  24.1 us
    all_gather x1, waiting for transfers between devices, on_device(): weight = lax.all_gather(out_weight.T, ('dp', 'ctx'), axis=0, tiled=True)  19.1 us
    pallas_call x1, Pallas kernels, project(): pl.pallas_call(project_kernel, grid=(features // tile,), in_specs=[pl.Blo...  17.3 us
    pallas_call x1, Pallas kernels, product_blocks(): pl.pallas_call(product_kernel, grid=(parts,), in_specs=[pl.BlockSpec((row...  10.1 us
    all_to_all x1, starting transfers between devices, on_device(): lax.all_to_all(product, 'ctx', split_axis=0, concat_axis=0, tiled=True)  8.43 us
    unnamed x8, local copies, waits for them, and re-layouts  8.24 us
  transfers between devices with their start and end apart: 2, of which 1 were waited for; matrix products, arithmetic and copies ran while one was open for 0% of the time, Pallas kernels for 35%

profile of v1, /device:TPU:1, one launch (start us, length us, event | category | flops | bytes accessed | tf_op | source)
XLA Modules:
  0.0 187.0 jit_solution(8069508071637689830)
XLA Ops:
  6.5 0.0 all-gather.2.cloned.1.call-start
  6.5 0.7 all-gather.2.cloned.1.call-update
  7.3 10.1 %product.1 = bf16[16,256,256]{2,1,0:T(8,128)(2,1)} custom-call(bf16[256,4096]{1,0:T(8,128)(2,1)} %bitcast.12, bf16[256,4096]{1,0:T(8,128)(2,1)} %bitcast.13), custom_call_target="tpu_custom_call" | custom-call | flops 1048576 | bytes 6291456 | tf_op jit(solution)/shard_map/product/pallas_call | solution.py:153
  17.3 8.4 %all-to-all-start = ((bf16[16,256,256]{2,1,0:T(8,128)(2,1)}), bf16[16,256,256]{2,1,0:T(8,128)(2,1)S(1)}, u32[]{:S(2)}, u32[]{:S(2)}) async-start(bf16[16,256,256]{2,1,0:T(8,128)(2,1)} %product.1), calls=%async_computation | async-start | bytes 4194304 | tf_op jit(solution)/shard_map/all_to_all | solution.py:372
  25.8 0.8 dynamic_slice.3
  26.5 0.0 copy-start
  26.6 2.2 %copy-done = bf16[32,256,256]{2,1,0:T(8,128)(2,1)S(1)} copy-done((bf16[32,256,256]{2,1,0:T(8,128)(2,1)S(1)}, bf16[32,256,256]{2,1,0:T(8,128)(2,1)}, u32[]{:S(2)}) %copy-start) | copy-done | bytes 4194328
  28.7 0.0 copy-start.1
  28.7 2.3 %copy-done.1 = bf16[32,256,256]{2,1,0:T(8,128)(2,1)S(1)} copy-done((bf16[32,256,256]{2,1,0:T(8,128)(2,1)S(1)}, bf16[32,256,256]{2,1,0:T(8,128)(2,1)}, u32[]{:S(2)}) %copy-start.1) | copy-done | bytes 4194328
  31.0 0.0 copy-start.2
  31.0 2.2 %copy-done.2 = f32[256,4096]{1,0:T(8,128)S(1)} copy-done((f32[256,4096]{1,0:T(8,128)S(1)}, f32[256,4096]{1,0:T(8,128)}, u32[]{:S(2)}) %copy-start.2) | copy-done | bytes 4194328
  33.2 24.1 %spectrum.1.spec_ref = f32[32,256,256]{2,1,0:T(8,128)} custom-call(f32[256,4096]{1,0:T(8,128)S(1)} %copy-done.2, bf16[32,256,256]{2,1,0:T(8,128)(2,1)S(1)} %copy-done, bf16[32,256,256]{2,1,0:T(8,128)(2,1)S(1)} %copy-done.1), custom_call_target="tpu_custom_call" | custom-call | flops 3221225472 | bytes 33554432 | tf_op jit(solution)/shard_map/spectrum/pallas_call | solution.py:205
  57.3 0.0 all-to-all-done
  57.3 30.5 %convolve.1 = bf16[4096,256]{1,0:T(8,128)(2,1)S(1)} custom-call(bf16[4096,256]{1,0:T(8,128)(2,1)S(1)} %bitcast.8, f32[32,256,256]{2,1,0:T(8,128)} %spectrum.1.spec_ref, f32[1,256]{1,0:T(1,128)S(1)} %bitcast.11, bf16[32,256,256]{2,1,0:T(8,128)(2,1)} %constant.18.clone.high_ref.fh_ref, bf16[32,256,256]{2,1,0:T(8,128)(2,1)} %constant.19.clone.low_ref.fl_ref, ...), custom_call_target="tpu_custom_call" | custom-call | flops 6442450944 | bytes 50331648 | tf_op jit(solution)/shard_map/convolve/pallas_call | solution.py:305
  87.9 54.3 %all_to_all.10.mixed_ref = bf16[16,256,256]{2,1,0:T(8,128)(2,1)S(1)} all-to-all(bf16[16,256,256]{2,1,0:T(8,128)(2,1)S(1)} %bitcast.9), channel_id=1, replica_groups=mesh['dp'=8,'ctx'=16] {'ctx'}, dimensions={0} | all-to-all | bytes 4194304 | tf_op jit(solution)/shard_map/all_to_all | solution.py:376
  142.2 19.1 %all-gather.2.cloned.1.call-done.weight_ref = bf16[4096,4096]{1,0:T(8,128)(2,1)} async-done(((bf16[32,4096]{1,0:T(8,128)(2,1)}), bf16[4096,4096]{1,0:T(8,128)(2,1)}) %all-gather.2.cloned.1.call-update) | async-done | bytes 33554448 | tf_op jit(solution)/shard_map/all_gather | solution.py:370
  161.2 0.0 copy-start.3
  161.2 1.6 copy-done.3
  162.8 17.3 %project.1 = bf16[256,4096]{1,0:T(8,128)(2,1)} custom-call(bf16[256,4096]{1,0:T(8,128)(2,1)S(1)} %bitcast.10, bf16[16,256,256]{2,1,0:T(8,128)(2,1)S(1)} %all_to_all.10.mixed_ref, bf16[4096,4096]{1,0:T(8,128)(2,1)} %all-gather.2.cloned.1.call-done.weight_ref), custom_call_target="tpu_custom_call" | custom-call | flops 8589934592 | bytes 33554432 | tf_op jit(solution)/shard_map/project/pallas_call | solution.py:346
Async XLA Ops:
  6.5 154.7 %all-gather.2.cloned.1.call-start = ((), (), s32[]{:S(2)}) async-start(), calls=%async_computation.2 | async-start | bytes 33816576 | tf_op jit(solution)/shard_map/all_gather | solution.py:370
  17.3 40.0 %all-to-all-start = ((bf16[16,256,256]{2,1,0:T(8,128)(2,1)}), bf16[16,256,256]{2,1,0:T(8,128)(2,1)S(1)}, u32[]{:S(2)}, u32[]{:S(2)}) async-start(bf16[16,256,256]{2,1,0:T(8,128)(2,1)} %product.1), calls=%async_computation | async-start | bytes 4194304 | tf_op jit(solution)/shard_map/all_to_all | solution.py:372
  26.5 2.2 %copy-start = (bf16[32,256,256]{2,1,0:T(8,128)(2,1)S(1)}, bf16[32,256,256]{2,1,0:T(8,128)(2,1)}, u32[]{:S(2)}) copy-start(bf16[32,256,256]{2,1,0:T(8,128)(2,1)} %constant.18.clone.high_ref.fh_ref) | copy-start | bytes 12582916
  28.7 2.3 %copy-start.1 = (bf16[32,256,256]{2,1,0:T(8,128)(2,1)S(1)}, bf16[32,256,256]{2,1,0:T(8,128)(2,1)}, u32[]{:S(2)}) copy-start(bf16[32,256,256]{2,1,0:T(8,128)(2,1)} %constant.19.clone.low_ref.fl_ref) | copy-start | bytes 12582916
  31.0 2.2 %copy-start.2 = (f32[256,4096]{1,0:T(8,128)S(1)}, f32[256,4096]{1,0:T(8,128)}, u32[]{:S(2)}) copy-start(f32[256,4096]{1,0:T(8,128)} %filters_ref.1) | copy-start | bytes 12582916
  161.2 1.6 copy-start.3
Sparse Core Ops, SparseCore 0:
  10.5 150.6 all-gather.1

commit v2 on v1

--- a/solution.py
+++ b/solution.py
@@ -15,6 +15,7 @@
 
 OUTER = 32
 INNER = 128
+CHUNKS = 4
 
 
 def split_table(table):
@@ -144,17 +145,21 @@
 
 
 def product_kernel(keys_ref, values_ref, out_ref):
-    out_ref[0] = (keys_ref[...].astype(F32) * values_ref[...].astype(F32)).astype(BF16)
+    parts, _, cols = out_ref.shape
+    for j in range(parts):
+        col = pl.ds(j * cols, cols)
+        out_ref[j] = (keys_ref[:, col].astype(F32) * values_ref[:, col].astype(F32)).astype(BF16)
 
 
 def product_blocks(keys, values, parts):
     rows, width = keys.shape
     cols = width // parts
+    tile = 64
     return pl.pallas_call(
         product_kernel,
-        grid=(parts,),
-        in_specs=[pl.BlockSpec((rows, cols), lambda j: (0, j))] * 2,
-        out_specs=pl.BlockSpec((1, rows, cols), lambda j: (j, 0, 0)),
+        grid=(rows // tile,),
+        in_specs=[pl.BlockSpec((tile, width), lambda j: (j, 0))] * 2,
+        out_specs=pl.BlockSpec((parts, tile, cols), lambda j: (0, j, 0)),
         out_shape=jax.ShapeDtypeStruct((parts, rows, cols), BF16),
         cost_estimate=pl.CostEstimate(flops=rows * width, bytes_accessed=6 * rows * width, transcendentals=0),
         name="product",
@@ -162,7 +167,7 @@
 
 
 def spectrum_kernel(filters_ref, high_ref, low_ref, out_ref, taps, high, low, sems):
-    chunks = 8
+    chunks = CHUNKS
     step = OUTER // chunks
 
     def fetch(i):
@@ -195,7 +200,7 @@
             out_ref[k] = close_dot(high[k], low[k], out_ref[k])
             return carry
 
-        lax.fori_loop(i * step, (i + 1) * step, inner, 0)
+        lax.fori_loop(i * step, (i + 1) * step, inner, 0, unroll=step)
 
 
 def filter_spectrum(filters, high, low):
@@ -216,7 +221,7 @@
             pltpu.VMEM((length, lanes), F32),
             pltpu.VMEM((OUTER, size, size), BF16),
             pltpu.VMEM((OUTER, size, size), BF16),
-            pltpu.SemaphoreType.DMA((2, 8)),
+            pltpu.SemaphoreType.DMA((2, CHUNKS)),
         ],
         compiler_params=pltpu.CompilerParams(vmem_limit_bytes=40 * MIB),
         cost_estimate=pl.CostEstimate(
@@ -229,7 +234,7 @@
 def conv_kernel(
     signal_ref, spec_ref, skip_ref, fh_ref, fl_ref, bh_ref, bl_ref, out_ref, work, spec, fh, fl, bh, bl, sems
 ):
-    chunks = 8
+    chunks = CHUNKS
     step = OUTER // chunks
     lanes = 128
     channels = out_ref.shape[1]
@@ -272,7 +277,7 @@
             work[k] = close_dot(bh[k], bl[k], mixed)
             return carry
 
-        lax.fori_loop(i * step, (i + 1) * step, inner, 0)
+        lax.fori_loop(i * step, (i + 1) * step, inner, 0, unroll=step)
 
     for c in range(0, channels, lanes):
         col = pl.ds(c, lanes)
@@ -314,7 +319,7 @@
             square,
             square,
             square,
-            pltpu.SemaphoreType.DMA((5, 8)),
+            pltpu.SemaphoreType.DMA((5, CHUNKS)),
         ],
         compiler_params=pltpu.CompilerParams(vmem_limit_bytes=48 * MIB),
         cost_estimate=pl.CostEstimate(

time: 188 us -> 179 us (0.952)
  waiting for transfers between devices: 19.8 us -> 62.4 us
  Pallas kernels: 82.1 us -> 54.1 us
  blocking collectives: 54.3 us -> 30.7 us
    all_gather x1, waiting for transfers between devices: 19.1 us -> 54 us  [on_device(): weight = lax.all_gather(out_weight.T, ('dp', 'ctx'), axis=0, tiled=True)]
    all_to_all x1, blocking collectives: 54.3 us -> 30.7 us  [on_device(): lax.all_to_all(mixed.reshape(count, rows, cols), 'ctx', split_axis=0, con...]
    pallas_call x1, Pallas kernels: 30.5 us -> 16.8 us  [convolve(): pl.pallas_call(conv_kernel, in_specs=[inside, anywhere, inside] + [anywhe...]
    pallas_call x1, Pallas kernels: 24.1 us -> 15.7 us  [filter_spectrum(): pl.pallas_call(spectrum_kernel, grid=(channels // lanes,), in_specs=[pl.B...]
    all_to_all x1, waiting for transfers between devices: 0.01 us -> 7.68 us  [on_device(): lax.all_to_all(product, 'ctx', split_axis=0, concat_axis=0, tiled=True)]
    pallas_call x1, Pallas kernels: 10.1 us -> 4.32 us  [product_blocks(): pl.pallas_call(product_kernel, grid=(rows // tile,), in_specs=[pl.BlockSp...]
  transfers between devices with their start and end apart: 2 -> 2, of which waited for: 1 -> 2; matrix products, arithmetic and copies ran while one was open for 0% -> 0% of each run, Pallas kernels for 35% -> 21%
where the time goes in v2:
time: 179 us; the launch traced here: 178 us
  waiting for transfers between devices  62.4 us (35%)
  Pallas kernels  54.1 us (30%)
  blocking collectives  30.7 us (17%)
  between operations  13.4 us (7%)
  local copies, waits for them, and re-layouts  9.09 us (5%)
  starting transfers between devices  8.43 us (5%)
    all_gather x1, waiting for transfers between devices, on_device(): weight = lax.all_gather(out_weight.T, ('dp', 'ctx'), axis=0, tiled=True)  54 us
    all_to_all x1, blocking collectives, on_device(): lax.all_to_all(mixed.reshape(count, rows, cols), 'ctx', split_axis=0, con...  30.7 us
    pallas_call x1, Pallas kernels, project(): pl.pallas_call(project_kernel, grid=(features // tile,), in_specs=[pl.Blo...  17.3 us
    pallas_call x1, Pallas kernels, convolve(): pl.pallas_call(conv_kernel, in_specs=[inside, anywhere, inside] + [anywhe...  16.8 us
    pallas_call x1, Pallas kernels, filter_spectrum(): pl.pallas_call(spectrum_kernel, grid=(channels // lanes,), in_specs=[pl.B...  15.7 us
    all_to_all x1, starting transfers between devices, on_device(): lax.all_to_all(product, 'ctx', split_axis=0, concat_axis=0, tiled=True)  8.43 us
    unnamed x8, local copies, waits for them, and re-layouts  8.32 us
    all_to_all x1, waiting for transfers between devices, on_device(): lax.all_to_all(product, 'ctx', split_axis=0, concat_axis=0, tiled=True)  7.68 us
  transfers between devices with their start and end apart: 2, of which 2 were waited for; matrix products, arithmetic and copies ran while one was open for 0% of the time, Pallas kernels for 21%

profile of v2, /device:TPU:1, one launch (start us, length us, event | category | flops | bytes accessed | tf_op | source)
XLA Modules:
  0.0 178.1 jit_solution(7981735431879562120)
XLA Ops:
  6.5 0.0 all-gather.2.cloned.1.call-start
  6.5 0.7 all-gather.2.cloned.1.call-update
  7.3 4.3 %product.1 = bf16[16,256,256]{2,1,0:T(8,128)(2,1)} custom-call(bf16[256,4096]{1,0:T(8,128)(2,1)} %bitcast.12, bf16[256,4096]{1,0:T(8,128)(2,1)} %bitcast.13), custom_call_target="tpu_custom_call" | custom-call | flops 1048576 | bytes 6291456 | tf_op jit(solution)/shard_map/product/pallas_call | solution.py:158
  11.6 8.4 %all-to-all-start = ((bf16[16,256,256]{2,1,0:T(8,128)(2,1)}), bf16[16,256,256]{2,1,0:T(8,128)(2,1)S(1)}, u32[]{:S(2)}, u32[]{:S(2)}) async-start(bf16[16,256,256]{2,1,0:T(8,128)(2,1)} %product.1), calls=%async_computation | async-start | bytes 4194304 | tf_op jit(solution)/shard_map/all_to_all | solution.py:377
  20.0 0.8 dynamic_slice.3
  20.8 0.0 copy-start
  20.8 2.2 %copy-done = bf16[32,256,256]{2,1,0:T(8,128)(2,1)S(1)} copy-done((bf16[32,256,256]{2,1,0:T(8,128)(2,1)S(1)}, bf16[32,256,256]{2,1,0:T(8,128)(2,1)}, u32[]{:S(2)}) %copy-start) | copy-done | bytes 4194328
  23.0 0.0 copy-start.1
  23.0 2.4 %copy-done.1 = bf16[32,256,256]{2,1,0:T(8,128)(2,1)S(1)} copy-done((bf16[32,256,256]{2,1,0:T(8,128)(2,1)S(1)}, bf16[32,256,256]{2,1,0:T(8,128)(2,1)}, u32[]{:S(2)}) %copy-start.1) | copy-done | bytes 4194328
  25.3 0.0 copy-start.2
  25.3 2.2 %copy-done.2 = f32[256,4096]{1,0:T(8,128)S(1)} copy-done((f32[256,4096]{1,0:T(8,128)S(1)}, f32[256,4096]{1,0:T(8,128)}, u32[]{:S(2)}) %copy-start.2) | copy-done | bytes 4194328
  27.5 15.7 %spectrum.1.spec_ref = f32[32,256,256]{2,1,0:T(8,128)} custom-call(f32[256,4096]{1,0:T(8,128)S(1)} %copy-done.2, bf16[32,256,256]{2,1,0:T(8,128)(2,1)S(1)} %copy-done, bf16[32,256,256]{2,1,0:T(8,128)(2,1)S(1)} %copy-done.1), custom_call_target="tpu_custom_call" | custom-call | flops 3221225472 | bytes 33554432 | tf_op jit(solution)/shard_map/spectrum/pallas_call | solution.py:210
  43.2 7.7 %all-to-all-done = bf16[16,256,256]{2,1,0:T(8,128)(2,1)S(1)} async-done(((bf16[16,256,256]{2,1,0:T(8,128)(2,1)}), bf16[16,256,256]{2,1,0:T(8,128)(2,1)S(1)}, u32[]{:S(2)}, u32[]{:S(2)}) %all-to-all-start) | async-done | bytes 2097184 | tf_op jit(solution)/shard_map/all_to_all | solution.py:377
  50.9 16.8 %convolve.1 = bf16[4096,256]{1,0:T(8,128)(2,1)S(1)} custom-call(bf16[4096,256]{1,0:T(8,128)(2,1)S(1)} %bitcast.8, f32[32,256,256]{2,1,0:T(8,128)} %spectrum.1.spec_ref, f32[1,256]{1,0:T(1,128)S(1)} %bitcast.11, bf16[32,256,256]{2,1,0:T(8,128)(2,1)} %constant.18.clone.high_ref.fh_ref, bf16[32,256,256]{2,1,0:T(8,128)(2,1)} %constant.19.clone.low_ref.fl_ref, ...), custom_call_target="tpu_custom_call" | custom-call | flops 6442450944 | bytes 50331648 | tf_op jit(solution)/shard_map/convolve/pallas_call | solution.py:310
  67.7 30.7 %all_to_all.10.mixed_ref = bf16[16,256,256]{2,1,0:T(8,128)(2,1)S(1)} all-to-all(bf16[16,256,256]{2,1,0:T(8,128)(2,1)S(1)} %bitcast.9), channel_id=1, replica_groups=mesh['dp'=8,'ctx'=16] {'ctx'}, dimensions={0} | all-to-all | bytes 4194304 | tf_op jit(solution)/shard_map/all_to_all | solution.py:381
  98.3 54.0 %all-gather.2.cloned.1.call-done.weight_ref = bf16[4096,4096]{1,0:T(8,128)(2,1)} async-done(((bf16[32,4096]{1,0:T(8,128)(2,1)}), bf16[4096,4096]{1,0:T(8,128)(2,1)}) %all-gather.2.cloned.1.call-update) | async-done | bytes 33554448 | tf_op jit(solution)/shard_map/all_gather | solution.py:375
  152.3 0.0 copy-start.3
  152.3 1.6 copy-done.3
  153.9 17.3 %project.1 = bf16[256,4096]{1,0:T(8,128)(2,1)} custom-call(bf16[256,4096]{1,0:T(8,128)(2,1)S(1)} %bitcast.10, bf16[16,256,256]{2,1,0:T(8,128)(2,1)S(1)} %all_to_all.10.mixed_ref, bf16[4096,4096]{1,0:T(8,128)(2,1)} %all-gather.2.cloned.1.call-done.weight_ref), custom_call_target="tpu_custom_call" | custom-call | flops 8589934592 | bytes 33554432 | tf_op jit(solution)/shard_map/project/pallas_call | solution.py:351
Async XLA Ops:
  6.5 145.8 %all-gather.2.cloned.1.call-start = ((), (), s32[]{:S(2)}) async-start(), calls=%async_computation.2 | async-start | bytes 33816576 | tf_op jit(solution)/shard_map/all_gather | solution.py:375
  11.6 39.3 %all-to-all-start = ((bf16[16,256,256]{2,1,0:T(8,128)(2,1)}), bf16[16,256,256]{2,1,0:T(8,128)(2,1)S(1)}, u32[]{:S(2)}, u32[]{:S(2)}) async-start(bf16[16,256,256]{2,1,0:T(8,128)(2,1)} %product.1), calls=%async_computation | async-start | bytes 4194304 | tf_op jit(solution)/shard_map/all_to_all | solution.py:377
  20.8 2.2 %copy-start = (bf16[32,256,256]{2,1,0:T(8,128)(2,1)S(1)}, bf16[32,256,256]{2,1,0:T(8,128)(2,1)}, u32[]{:S(2)}) copy-start(bf16[32,256,256]{2,1,0:T(8,128)(2,1)} %constant.18.clone.high_ref.fh_ref) | copy-start | bytes 12582916
  23.0 2.4 %copy-start.1 = (bf16[32,256,256]{2,1,0:T(8,128)(2,1)S(1)}, bf16[32,256,256]{2,1,0:T(8,128)(2,1)}, u32[]{:S(2)}) copy-start(bf16[32,256,256]{2,1,0:T(8,128)(2,1)} %constant.19.clone.low_ref.fl_ref) | copy-start | bytes 12582916
  25.3 2.2 %copy-start.2 = (f32[256,4096]{1,0:T(8,128)S(1)}, f32[256,4096]{1,0:T(8,128)}, u32[]{:S(2)}) copy-start(f32[256,4096]{1,0:T(8,128)} %filters_ref.1) | copy-start | bytes 12582916
  152.3 1.6 copy-start.3
Sparse Core Ops, SparseCore 0:
  10.5 141.7 all-gather.1

commit v3 on v2

--- a/solution.py
+++ b/solution.py
@@ -7,6 +7,7 @@
 from jax import lax
 from jax.experimental import pallas as pl
 from jax.experimental.pallas import tpu as pltpu
+from jax.sharding import Mesh
 from jax.sharding import PartitionSpec as P
 
 F32 = jnp.float32
@@ -329,68 +330,151 @@
     )(signal, spec, skip, *table)
 
 
-def project_kernel(queries_ref, mixed_ref, weight_ref, out_ref, gated):
-    parts = mixed_ref.shape[0]
-    width = mixed_ref.shape[2]
-
-    @pl.when(pl.program_id(0) == 0)
+def project_kernel(place_ref, queries_ref, mixed_ref, weight_ref, *rest):
+    tiles = group_tiles(rest[:-4])
+    out_ref, gated, held, sems = rest[-4:]
+    parts, _, width = mixed_ref.shape
+    depth = weight_ref.shape[1]
+    step = pl.program_id(0)
+    half = held.shape[1] // 2
+
+    def copies(i):
+        slot = held.at[i % 2]
+        if len(tiles[i]) == 1:
+            return [pltpu.make_async_copy(tiles[i][0], slot, sems.at[i % 2, 0])]
+        return [
+            pltpu.make_async_copy(part, slot.at[pl.ds(h * half, half)], sems.at[i % 2, h])
+            for h, part in enumerate(tiles[i])
+        ]
+
+    count = len(tiles)
+
+    @pl.when(step == 0)
     def _():
+        for copy in copies(0):
+            copy.start()
         for j in range(parts):
             cols = pl.ds(j * width, width)
             gated[:, cols] = (queries_ref[:, cols].astype(F32) * mixed_ref[j].astype(F32)).astype(BF16)
 
-    out_ref[...] = lax.dot_general(
-        gated[...], weight_ref[...], (((1,), (1,)), ((), ())), preferred_element_type=F32
-    ).astype(BF16)
-
-
-def project(queries, mixed, weight):
+    for i in range(count):
+
+        @pl.when(step == i)
+        def _():
+            if i + 1 < count:
+                for copy in copies(i + 1):
+                    copy.start()
+            for copy in copies(i):
+                copy.wait()
+            dims = (((1,), (1,)), ((), ()))
+            first = lax.dot_general(gated[:, :depth], weight_ref[...], dims, preferred_element_type=F32)
+            second = lax.dot_general(gated[:, depth:], held[i % 2], dims, preferred_element_type=F32)
+            out_ref[...] = (first + second).astype(BF16)
+
+
+def group_tiles(refs):
+    groups = []
+    for base in (0, 5):
+        own, back, ahead, far_low, far_high = refs[base : base + 5]
+        groups += [(own,), (back,), (ahead,), (far_low, far_high)]
+    return groups
+
+
+def project(queries, mixed, weight, tiles, place):
     rows, width = queries.shape
-    features = weight.shape[0]
-    tile = 512
+    features, depth = weight.shape
+    tile, rest = tiles[0].shape
     return pl.pallas_call(
         project_kernel,
-        grid=(features // tile,),
-        in_specs=[
-            pl.BlockSpec((rows, width), lambda n: (0, 0)),
-            pl.BlockSpec(mixed.shape, lambda n: (0, 0, 0)),
-            pl.BlockSpec((tile, width), lambda n: (n, 0)),
-        ],
-        out_specs=pl.BlockSpec((rows, tile), lambda n: (0, n)),
+        grid_spec=pltpu.PrefetchScalarGridSpec(
+            num_scalar_prefetch=1,
+            grid=(features // tile,),
+            in_specs=[
+                pl.BlockSpec((rows, width), lambda n, place: (0, 0)),
+                pl.BlockSpec(mixed.shape, lambda n, place: (0, 0, 0)),
+                pl.BlockSpec((tile, depth), lambda n, place: (place[n], 0)),
+            ]
+            + [pl.BlockSpec(memory_space=pl.ANY)] * len(tiles),
+            out_specs=pl.BlockSpec((rows, tile), lambda n, place: (0, place[n])),
+            scratch_shapes=[
+                pltpu.VMEM((rows, width), BF16),
+                pltpu.VMEM((2, tile, rest), BF16),
+                pltpu.SemaphoreType.DMA((2, 2)),
+            ],
+        ),
         out_shape=jax.ShapeDtypeStruct((rows, features), BF16),
-        scratch_shapes=[pltpu.VMEM((rows, width), BF16)],
         compiler_params=pltpu.CompilerParams(vmem_limit_bytes=40 * MIB),
         cost_estimate=pl.CostEstimate(
             flops=2 * rows * width * features, bytes_accessed=2 * width * features, transcendentals=0
         ),
         name="project",
-    )(queries, mixed, weight)
+    )(place, queries, mixed, weight, *tiles)
+
+
+def around(block, axis):
+    size = lax.axis_size(axis)
+    half = block.shape[0] // 2
+    up = [(i, (i + 1) % size) for i in range(size)]
+    down = [(i, (i - 1) % size) for i in range(size)]
+    back = lax.ppermute(block, axis, up)
+    ahead = lax.ppermute(block, axis, down)
+    far_low = lax.ppermute(back[:half], axis, up)
+    far_high = lax.ppermute(ahead[half:], axis, down)
+    return block, back, ahead, far_low, far_high
+
+
+def gather_ring(block, axis):
+    size = lax.axis_size(axis)
+    me = lax.axis_index(axis)
+    rows = block.shape[0]
+    own, back, ahead, far_low, far_high = around(block, axis)
+    whole = jnp.zeros((size * rows, block.shape[1]), block.dtype)
+    for piece, shift, offset in ((own, 0, 0), (back, -1, 0), (ahead, 1, 0), (far_low, 2, 0), (far_high, 2, rows // 2)):
+        start = (me + shift + size) % size * rows + offset
+        whole = lax.dynamic_update_slice_in_dim(whole, piece, start, 0)
+    return whole
+
+
+def gather_tiles(block):
+    plane = gather_ring(gather_ring(block, "z"), "x")
+    mine = around(plane, "y")
+    others = [lax.ppermute(piece, "core", [(0, 1), (1, 0)]) for piece in mine]
+    y, core = lax.axis_index("y"), lax.axis_index("core")
+    count = lax.axis_size("y")
+    place = [(y + shift + count) % count * 2 + c for c in (core, 1 - core) for shift in (0, -1, 1, 2)]
+    return list(mine) + others, jnp.stack(place).astype(jnp.int32)
 
 
 def on_device(queries, keys_in, values_in, filters, skip_gain, out_weight):
-    count = lax.axis_size("ctx")
+    ctx = ("x", "z")
+    count = lax.axis_size(ctx)
     rows, width = queries.shape[1:]
     cols = width // count
+    depth = width // 2
     table = [jnp.asarray(t) for t in tables()]
-    weight = lax.all_gather(out_weight.T, ("dp", "ctx"), axis=0, tiled=True)
+    turned = out_weight.T
+    weight = lax.all_gather(turned[:, :depth], ("y", "core", "x", "z"), axis=0, tiled=True)
+    tiles, place = gather_tiles(turned[:, depth:])
     product = product_blocks(keys_in[0], values_in[0], count)
-    piece = lax.all_to_all(product, "ctx", split_axis=0, concat_axis=0, tiled=True)
+    piece = lax.all_to_all(product, ctx, split_axis=0, concat_axis=0, tiled=True)
     spec = filter_spectrum(filters, table[0], table[1])
-    skip = lax.dynamic_slice_in_dim(skip_gain, lax.axis_index("ctx") * cols, cols).reshape(1, cols)
+    skip = lax.dynamic_slice_in_dim(skip_gain, lax.axis_index(ctx) * cols, cols).reshape(1, cols)
     mixed = convolve(piece.reshape(count * rows, cols), spec, skip, table)
-    returned = lax.all_to_all(mixed.reshape(count, rows, cols), "ctx", split_axis=0, concat_axis=0, tiled=True)
-    return project(queries[0], returned, weight)[None]
+    returned = lax.all_to_all(mixed.reshape(count, rows, cols), ctx, split_axis=0, concat_axis=0, tiled=True)
+    return project(queries[0], returned, weight, tiles, place)[None]
 
 
 def solution(mesh):
+    chips = Mesh(mesh.devices.reshape(4, 2, 4, 4), ("y", "core", "x", "z"))
+    dp, ctx = ("y", "core"), ("x", "z")
     in_specs = (
-        P("dp", "ctx", None),
-        P("dp", "ctx", None),
-        P("dp", "ctx", None),
-        P("ctx", None),
+        P(dp, ctx, None),
+        P(dp, ctx, None),
+        P(dp, ctx, None),
+        P(ctx, None),
         P(),
-        P(None, ("dp", "ctx")),
+        P(None, dp + ctx),
     )
     return jax.shard_map(
-        on_device, mesh=mesh, in_specs=in_specs, out_specs=P("dp", "ctx", None), check_vma=False
+        on_device, mesh=chips, in_specs=in_specs, out_specs=P(dp, ctx, None), check_vma=False
     )

time: 179 us -> 206 us (1.15)
  starting transfers between devices: 8.43 us -> 49.5 us
  blocking collectives: 30.7 us -> 0 us
  local copies, waits for them, and re-layouts: 9.09 us -> 21.1 us
  Pallas kernels: 54.1 us -> 56.4 us
    all_gather x1, waiting for transfers between devices: 54 us -> 0.02 us  [on_device(): lax.all_gather(turned[:, :depth], ('y', 'core', 'x', 'z'), axis=0, tiled=...]
    ppermute x0 -> x17, starting transfers between devices: none -> 37.2 us  [the longest x5 18 us: gather_tiles(): others = [lax.ppermute(piece, 'core', [(0, 1), (1, 0)]) for piece in mine]]
    ppermute x0 -> x17, waiting for transfers between devices: none -> 36.1 us  [the longest x3 32.8 us: around(): back = lax.ppermute(block, axis, up)]
    all_to_all x1 -> x0, blocking collectives: 30.7 us -> none  [on_device(): lax.all_to_all(mixed.reshape(count, rows, cols), 'ctx', split_axis=0, con...]
    all_to_all x1 -> x2, waiting for transfers between devices: 7.68 us -> 27.6 us  [the longest x1 27.6 us: on_device(): lax.all_to_all(mixed.reshape(count, rows, cols), ctx, split_axis=0, conca...]
    slice x0 -> x7, local copies, waits for them, and re-layouts: none -> 6.33 us  [the longest x3 2.33 us: around(): far_high = lax.ppermute(ahead[half:], axis, down)]
    dynamic_update_slice x0 -> x9, local copies, waits for them, and re-layouts: none -> 4.02 us  [gather_ring(): whole = lax.dynamic_update_slice_in_dim(whole, piece, start, 0)]
    all_to_all x1 -> x2, starting transfers between devices: 8.43 us -> 12.4 us  [the longest x1 6.23 us: on_device(): lax.all_to_all(product, ctx, split_axis=0, concat_axis=0, tiled=True)]
  transfers between devices with their start and end apart: 2 -> 20, of which waited for: 2 -> 6; matrix products, arithmetic and copies ran while one was open for 0% -> 5% of each run, Pallas kernels for 21% -> 19%
where the time goes in v3:
time: 206 us; the launch traced here: 204 us
  waiting for transfers between devices  63.8 us (31%)
  Pallas kernels  56.4 us (27%)
  starting transfers between devices  49.5 us (24%)
  local copies, waits for them, and re-layouts  21.1 us (10%)
  between operations  13.6 us (7%)
    ppermute x3, waiting for transfers between devices, around(): back = lax.ppermute(block, axis, up)  32.8 us
    all_to_all x1, waiting for transfers between devices, on_device(): lax.all_to_all(mixed.reshape(count, rows, cols), ctx, split_axis=0, conca...  27.6 us
    pallas_call x1, Pallas kernels, project(): pl.pallas_call(project_kernel, grid_spec=pltpu.PrefetchScalarGridSpec(num...  18.4 us
    ppermute x5, starting transfers between devices, gather_tiles(): others = [lax.ppermute(piece, 'core', [(0, 1), (1, 0)]) for piece in mine]  18 us
    pallas_call x1, Pallas kernels, convolve(): pl.pallas_call(conv_kernel, in_specs=[inside, anywhere, inside] + [anywhe...  17.9 us
    pallas_call x1, Pallas kernels, filter_spectrum(): pl.pallas_call(spectrum_kernel, grid=(channels // lanes,), in_specs=[pl.B...  15.7 us
    unnamed x8, local copies, waits for them, and re-layouts  8.19 us
    ppermute x3, starting transfers between devices, around(): far_high = lax.ppermute(ahead[half:], axis, down)  7.71 us
  transfers between devices with their start and end apart: 20, of which 6 were waited for; matrix products, arithmetic and copies ran while one was open for 5% of the time, Pallas kernels for 19%

profile of v3, /device:TPU:1, one launch (start us, length us, event | category | flops | bytes accessed | tf_op | source)
XLA Modules:
  0.0 204.4 jit_solution(8787151590031619594)
XLA Ops:
  6.6 1.7 fusion
  8.3 2.5 %collective-permute-start = (bf16[32,2048]{1,0:T(8,128)(2,1)S(1)}, bf16[32,2048]{1,0:T(8,128)(2,1)S(1)}, u32[]{:S(2)}, u32[]{:S(2)}) collective-permute-start(bf16[32,2048]{1,0:T(8,128)(2,1)S(1)} %get-tuple-element.5), channel_id=1, source_target_pairs={{0,1},{1,2},{2,3},{3,0},{4,5},{5,6},{6,7},{7,4},{8,9},{9,10},{10,1... | collective-permute-start | bytes 393224 | tf_op jit(solution)/shard_map/ppermute | solution.py:419
  10.8 2.2 %collective-permute-start.1 = (bf16[32,2048]{1,0:T(8,128)(2,1)S(1)}, bf16[32,2048]{1,0:T(8,128)(2,1)S(1)}, u32[]{:S(2)}, u32[]{:S(2)}) collective-permute-start(bf16[32,2048]{1,0:T(8,128)(2,1)S(1)} %get-tuple-element.5), channel_id=1, source_target_pairs={{0,3},{1,0},{2,1},{3,2},{4,7},{5,4},{6,5},{7,6},{8,11},{9,8},{10,9... | collective-permute-start | bytes 393224 | tf_op jit(solution)/shard_map/ppermute | solution.py:420
  13.0 3.1 %collective-permute-done = bf16[32,2048]{1,0:T(8,128)(2,1)S(1)} collective-permute-done((bf16[32,2048]{1,0:T(8,128)(2,1)S(1)}, bf16[32,2048]{1,0:T(8,128)(2,1)S(1)}, u32[]{:S(2)}, u32[]{:S(2)}) %collective-permute-start) | collective-permute-done | bytes 131104 | tf_op jit(solution)/shard_map/ppermute | solution.py:419
  16.2 2.7 %collective-permute-start.3 = (bf16[16,2048]{1,0:T(8,128)(2,1)S(1)}, bf16[16,2048]{1,0:T(8,128)(2,1)S(1)}, u32[]{:S(2)}, u32[]{:S(2)}) collective-permute-start(bf16[16,2048]{1,0:T(8,128)(2,1)S(1)} %slice.35), channel_id=1, source_target_pairs={{0,3},{1,0},{2,1},{3,2},{4,7},{5,4},{6,5},{7,6},{8,11},{9,8},{10,9... | collective-permute-start | bytes 196616 | tf_op jit(solution)/shard_map/ppermute | solution.py:422
  25.7 7.9 %collective-permute-done.4 = bf16[128,2048]{1,0:T(8,128)(2,1)S(1)} collective-permute-done((bf16[128,2048]{1,0:T(8,128)(2,1)S(1)}, bf16[128,2048]{1,0:T(8,128)(2,1)S(1)}, u32[]{:S(2)}, u32[]{:S(2)}) %collective-permute-start.4) | collective-permute-done | bytes 524320 | tf_op jit(solution)/shard_map/ppermute | solution.py:419
  34.1 2.9 %collective-permute-start.7 = (bf16[64,2048]{1,0:T(8,128)(2,1)S(1)}, bf16[64,2048]{1,0:T(8,128)(2,1)S(1)}, u32[]{:S(2)}, u32[]{:S(2)}) collective-permute-start(bf16[64,2048]{1,0:T(8,128)(2,1)S(1)} %slice.37), channel_id=1, source_target_pairs={{0,12},{4,0},{8,4},{12,8},{1,13},{5,1},{9,5},{13,9},{2,14},{6,2},{... | collective-permute-start | bytes 786440 | tf_op jit(solution)/shard_map/ppermute | solution.py:422
  38.6 1.8 collective-permute-done.6
  44.5 4.3 %product.1 = bf16[16,256,256]{2,1,0:T(8,128)(2,1)} custom-call(bf16[256,4096]{1,0:T(8,128)(2,1)} %bitcast.19, bf16[256,4096]{1,0:T(8,128)(2,1)} %bitcast.20), custom_call_target="tpu_custom_call" | custom-call | flops 1048576 | bytes 6291456 | tf_op jit(solution)/shard_map/product/pallas_call | solution.py:159
  48.9 6.2 %all-to-all-start = ((bf16[16,256,256]{2,1,0:T(8,128)(2,1)}), bf16[16,256,256]{2,1,0:T(8,128)(2,1)S(1)}, u32[]{:S(2)}, u32[]{:S(2)}) async-start(bf16[16,256,256]{2,1,0:T(8,128)(2,1)} %product.1), calls=%async_computation | async-start | bytes 4194304 | tf_op jit(solution)/shard_map/all_to_all | solution.py:459
  55.9 2.2 %copy-done = bf16[32,256,256]{2,1,0:T(8,128)(2,1)S(1)} copy-done((bf16[32,256,256]{2,1,0:T(8,128)(2,1)S(1)}, bf16[32,256,256]{2,1,0:T(8,128)(2,1)}, u32[]{:S(2)}) %copy-start) | copy-done | bytes 4194328
  58.1 2.2 %copy-done.1 = bf16[32,256,256]{2,1,0:T(8,128)(2,1)S(1)} copy-done((bf16[32,256,256]{2,1,0:T(8,128)(2,1)S(1)}, bf16[32,256,256]{2,1,0:T(8,128)(2,1)}, u32[]{:S(2)}) %copy-start.1) | copy-done | bytes 4194328
  60.3 2.2 %copy-done.2 = f32[256,4096]{1,0:T(8,128)S(1)} copy-done((f32[256,4096]{1,0:T(8,128)S(1)}, f32[256,4096]{1,0:T(8,128)}, u32[]{:S(2)}) %copy-start.2) | copy-done | bytes 4194328
  62.5 15.7 %spectrum.1.spec_ref = f32[32,256,256]{2,1,0:T(8,128)} custom-call(f32[256,4096]{1,0:T(8,128)S(1)} %copy-done.2, bf16[32,256,256]{2,1,0:T(8,128)(2,1)S(1)} %copy-done, bf16[32,256,256]{2,1,0:T(8,128)(2,1)S(1)} %copy-done.1), custom_call_target="tpu_custom_call" | custom-call | flops 3221225472 | bytes 33554432 | tf_op jit(solution)/shard_map/spectrum/pallas_call | solution.py:211
  78.2 5.6 %collective-permute-start.12 = (bf16[512,2048]{1,0:T(8,128)(2,1)}, bf16[512,2048]{1,0:T(8,128)(2,1)}, u32[]{:S(2)}, u32[]{:S(2)}) collective-permute-start(bf16[512,2048]{1,0:T(8,128)(2,1)} %constant_dynamic-update-slice_fusion.rest_0_), channel_id=1, source_target_pairs={{0,16},{16,0},{1,17},{17,1},{2,18},{18,2},{3,19},{19,3},{4,20},{20... | collective-permute-start | bytes 6291464 | tf_op jit(solution)/shard_map/ppermute | solution.py:441
  83.9 21.7 %collective-permute-done.8.rest_1_ = bf16[512,2048]{1,0:T(8,128)(2,1)} collective-permute-done((bf16[512,2048]{1,0:T(8,128)(2,1)}, bf16[512,2048]{1,0:T(8,128)(2,1)}, u32[]{:S(2)}, u32[]{:S(2)}) %collective-permute-start.8) | collective-permute-done | bytes 2097184 | tf_op jit(solution)/shard_map/ppermute | solution.py:419
  105.5 2.3 %slice.38 = bf16[256,2048]{1,0:T(8,128)(2,1)} slice(bf16[512,2048]{1,0:T(8,128)(2,1)} %collective-permute-done.8.rest_1_), slice={[0:256], [0:2048]} | slice | bytes 2097152 | tf_op jit(solution)/shard_map/slice | solution.py:421
  108.8 2.3 %slice.39 = bf16[256,2048]{1,0:T(8,128)(2,1)} slice(bf16[512,2048]{1,0:T(8,128)(2,1)} %collective-permute-done.9.rest_2_), slice={[256:512], [0:2048]} | slice | bytes 2097152 | tf_op jit(solution)/shard_map/slice | solution.py:422
  111.1 2.1 %collective-permute-start.11 = (bf16[256,2048]{1,0:T(8,128)(2,1)}, bf16[256,2048]{1,0:T(8,128)(2,1)}, u32[]{:S(2)}, u32[]{:S(2)}) collective-permute-start(bf16[256,2048]{1,0:T(8,128)(2,1)} %slice.39), channel_id=1, source_target_pairs={{0,96},{32,0},{64,32},{96,64},{1,97},{33,1},{65,33},{97,65},{2,98}... | collective-permute-start | bytes 3145736 | tf_op jit(solution)/shard_map/ppermute | solution.py:422
  113.2 11.2 %collective-permute-start.13 = (bf16[512,2048]{1,0:T(8,128)(2,1)}, bf16[512,2048]{1,0:T(8,128)(2,1)}, u32[]{:S(2)}, u32[]{:S(2)}) collective-permute-start(bf16[512,2048]{1,0:T(8,128)(2,1)} %collective-permute-done.8.rest_1_), channel_id=1, source_target_pairs={{0,16},{16,0},{1,17},{17,1},{2,18},{18,2},{3,19},{19,3},{4,20},{20... | collective-permute-start | bytes 6291464 | tf_op jit(solution)/shard_map/ppermute | solution.py:441
  124.4 17.9 %convolve.1 = bf16[4096,256]{1,0:T(8,128)(2,1)} custom-call(bf16[4096,256]{1,0:T(8,128)(2,1)S(1)} %bitcast.16, f32[32,256,256]{2,1,0:T(8,128)} %spectrum.1.spec_ref, f32[1,256]{1,0:T(1,128)S(1)} %bitcast.18, bf16[32,256,256]{2,1,0:T(8,128)(2,1)} %constant.132.clone.high_ref.fh_ref, bf16[32,256,256]{2,1,0:T(8,128)(2,1)} %constant.133.clone.low_ref.fl_ref, ...), custom_call_target="tpu_custom_call" | custom-call | flops 6442450944 | bytes 50331648 | tf_op jit(solution)/shard_map/convolve/pallas_call | solution.py:311
  142.4 6.1 %all-to-all-start.1 = ((bf16[16,256,256]{2,1,0:T(8,128)(2,1)}), bf16[16,256,256]{2,1,0:T(8,128)(2,1)S(1)}, u32[]{:S(2)}, u32[]{:S(2)}) async-start(bf16[16,256,256]{2,1,0:T(8,128)(2,1)} %bitcast.13), calls=%async_computation.1 | async-start | bytes 4194304 | tf_op jit(solution)/shard_map/all_to_all | solution.py:463
  149.8 27.6 %all-to-all-done.1.mixed_ref = bf16[16,256,256]{2,1,0:T(8,128)(2,1)S(1)} async-done(((bf16[16,256,256]{2,1,0:T(8,128)(2,1)}), bf16[16,256,256]{2,1,0:T(8,128)(2,1)S(1)}, u32[]{:S(2)}, u32[]{:S(2)}) %all-to-all-start.1) | async-done | bytes 2097184 | tf_op jit(solution)/shard_map/all_to_all | solution.py:463
  179.1 18.4 %project.1 = bf16[256,4096]{1,0:T(8,128)(2,1)} custom-call(s32[8]{0:T(128)S(1)} %stack.35.place_ref, bf16[256,4096]{1,0:T(8,128)(2,1)S(1)} %bitcast.17, bf16[16,256,256]{2,1,0:T(8,128)(2,1)S(1)} %all-to-all-done.1.mixed_ref, bf16[4096,2048]{1,0:T(8,128)(2,1)} %all-gather.2.cloned.1.call-done.weight_ref, ...), custom_call_target="tpu_custom_call" | custom-call | flops 8589934592 | bytes 33554432 | tf_op jit(solution)/shard_map/project/pallas_call | solution.py:387
  (49 shorter events, 17.7 us)
Async XLA Ops:
  6.5 170.9 %all-gather.2.cloned.1.call-start = ((), (), s32[]{:S(2)}) async-start(), calls=%async_computation.2 | async-start | bytes 16908288 | tf_op jit(solution)/shard_map/all_gather | solution.py:456
  8.3 7.9 %collective-permute-start = (bf16[32,2048]{1,0:T(8,128)(2,1)S(1)}, bf16[32,2048]{1,0:T(8,128)(2,1)S(1)}, u32[]{:S(2)}, u32[]{:S(2)}) collective-permute-start(bf16[32,2048]{1,0:T(8,128)(2,1)S(1)} %get-tuple-element.5), channel_id=1, source_target_pairs={{0,1},{1,2},{2,3},{3,0},{4,5},{5,6},{6,7},{7,4},{8,9},{9,10},{10,1... | collective-permute-start | bytes 393224 | tf_op jit(solution)/shard_map/ppermute | solution.py:419
  10.8 5.4 %collective-permute-start.1 = (bf16[32,2048]{1,0:T(8,128)(2,1)S(1)}, bf16[32,2048]{1,0:T(8,128)(2,1)S(1)}, u32[]{:S(2)}, u32[]{:S(2)}) collective-permute-start(bf16[32,2048]{1,0:T(8,128)(2,1)S(1)} %get-tuple-element.5), channel_id=1, source_target_pairs={{0,3},{1,0},{2,1},{3,2},{4,7},{5,4},{6,5},{7,6},{8,11},{9,8},{10,9... | collective-permute-start | bytes 393224 | tf_op jit(solution)/shard_map/ppermute | solution.py:420
  16.2 4.3 %collective-permute-start.2 = (bf16[16,2048]{1,0:T(8,128)(2,1)S(1)}, bf16[16,2048]{1,0:T(8,128)(2,1)S(1)}, u32[]{:S(2)}, u32[]{:S(2)}) collective-permute-start(bf16[16,2048]{1,0:T(8,128)(2,1)S(1)} %slice.34), channel_id=1, source_target_pairs={{0,1},{1,2},{2,3},{3,0},{4,5},{5,6},{6,7},{7,4},{8,9},{9,10},{10,1... | collective-permute-start | bytes 196616 | tf_op jit(solution)/shard_map/ppermute | solution.py:421
  16.2 4.3 %collective-permute-start.3 = (bf16[16,2048]{1,0:T(8,128)(2,1)S(1)}, bf16[16,2048]{1,0:T(8,128)(2,1)S(1)}, u32[]{:S(2)}, u32[]{:S(2)}) collective-permute-start(bf16[16,2048]{1,0:T(8,128)(2,1)S(1)} %slice.35), channel_id=1, source_target_pairs={{0,3},{1,0},{2,1},{3,2},{4,7},{5,4},{6,5},{7,6},{8,11},{9,8},{10,9... | collective-permute-start | bytes 196616 | tf_op jit(solution)/shard_map/ppermute | solution.py:422
  20.5 13.1 %collective-permute-start.4 = (bf16[128,2048]{1,0:T(8,128)(2,1)S(1)}, bf16[128,2048]{1,0:T(8,128)(2,1)S(1)}, u32[]{:S(2)}, u32[]{:S(2)}) collective-permute-start(bf16[128,2048]{1,0:T(8,128)(2,1)S(1)} %constant_dynamic-update-slice_fusion.5), channel_id=1, source_target_pairs={{0,4},{4,8},{8,12},{12,0},{1,5},{5,9},{9,13},{13,1},{2,6},{6,10},{... | collective-permute-start | bytes 1572872 | tf_op jit(solution)/shard_map/ppermute | solution.py:419
  21.8 12.2 %collective-permute-start.5 = (bf16[128,2048]{1,0:T(8,128)(2,1)S(1)}, bf16[128,2048]{1,0:T(8,128)(2,1)S(1)}, u32[]{:S(2)}, u32[]{:S(2)}) collective-permute-start(bf16[128,2048]{1,0:T(8,128)(2,1)S(1)} %constant_dynamic-update-slice_fusion.5), channel_id=1, source_target_pairs={{0,12},{4,0},{8,4},{12,8},{1,13},{5,1},{9,5},{13,9},{2,14},{6,2},{... | collective-permute-start | bytes 1572872 | tf_op jit(solution)/shard_map/ppermute | solution.py:420
  33.7 6.7 %collective-permute-start.6 = (bf16[64,2048]{1,0:T(8,128)(2,1)S(1)}, bf16[64,2048]{1,0:T(8,128)(2,1)S(1)}, u32[]{:S(2)}, u32[]{:S(2)}) collective-permute-start(bf16[64,2048]{1,0:T(8,128)(2,1)S(1)} %slice.36), channel_id=1, source_target_pairs={{0,4},{4,8},{8,12},{12,0},{1,5},{5,9},{9,13},{13,1},{2,6},{6,10},{... | collective-permute-start | bytes 786440 | tf_op jit(solution)/shard_map/ppermute | solution.py:421
  34.1 7.1 %collective-permute-start.7 = (bf16[64,2048]{1,0:T(8,128)(2,1)S(1)}, bf16[64,2048]{1,0:T(8,128)(2,1)S(1)}, u32[]{:S(2)}, u32[]{:S(2)}) collective-permute-start(bf16[64,2048]{1,0:T(8,128)(2,1)S(1)} %slice.37), channel_id=1, source_target_pairs={{0,12},{4,0},{8,4},{12,8},{1,13},{5,1},{9,5},{13,9},{2,14},{6,2},{... | collective-permute-start | bytes 786440 | tf_op jit(solution)/shard_map/ppermute | solution.py:422
  41.9 63.7 %collective-permute-start.8 = (bf16[512,2048]{1,0:T(8,128)(2,1)}, bf16[512,2048]{1,0:T(8,128)(2,1)}, u32[]{:S(2)}, u32[]{:S(2)}) collective-permute-start(bf16[512,2048]{1,0:T(8,128)(2,1)} %constant_dynamic-update-slice_fusion.rest_0_), channel_id=1, source_target_pairs={{0,32},{32,64},{64,96},{96,0},{1,33},{33,65},{65,97},{97,1},{2,34}... | collective-permute-start | bytes 6291464 | tf_op jit(solution)/shard_map/ppermute | solution.py:419
  43.1 65.7 %collective-permute-start.9 = (bf16[512,2048]{1,0:T(8,128)(2,1)}, bf16[512,2048]{1,0:T(8,128)(2,1)}, u32[]{:S(2)}, u32[]{:S(2)}) collective-permute-start(bf16[512,2048]{1,0:T(8,128)(2,1)} %constant_dynamic-update-slice_fusion.rest_0_), channel_id=1, source_target_pairs={{0,96},{32,0},{64,32},{96,64},{1,97},{33,1},{65,33},{97,65},{2,98}... | collective-permute-start | bytes 6291464 | tf_op jit(solution)/shard_map/ppermute | solution.py:420
  48.9 75.5 %all-to-all-start = ((bf16[16,256,256]{2,1,0:T(8,128)(2,1)}), bf16[16,256,256]{2,1,0:T(8,128)(2,1)S(1)}, u32[]{:S(2)}, u32[]{:S(2)}) async-start(bf16[16,256,256]{2,1,0:T(8,128)(2,1)} %product.1), calls=%async_computation | async-start | bytes 4194304 | tf_op jit(solution)/shard_map/all_to_all | solution.py:459
  55.9 2.2 %copy-start = (bf16[32,256,256]{2,1,0:T(8,128)(2,1)S(1)}, bf16[32,256,256]{2,1,0:T(8,128)(2,1)}, u32[]{:S(2)}) copy-start(bf16[32,256,256]{2,1,0:T(8,128)(2,1)} %constant.132.clone.high_ref.fh_ref) | copy-start | bytes 12582916
  58.1 2.2 %copy-start.1 = (bf16[32,256,256]{2,1,0:T(8,128)(2,1)S(1)}, bf16[32,256,256]{2,1,0:T(8,128)(2,1)}, u32[]{:S(2)}) copy-start(bf16[32,256,256]{2,1,0:T(8,128)(2,1)} %constant.133.clone.low_ref.fl_ref) | copy-start | bytes 12582916
  60.3 2.2 %copy-start.2 = (f32[256,4096]{1,0:T(8,128)S(1)}, f32[256,4096]{1,0:T(8,128)}, u32[]{:S(2)}) copy-start(f32[256,4096]{1,0:T(8,128)} %filters_ref.1) | copy-start | bytes 12582916
  78.2 71.6 %collective-permute-start.12 = (bf16[512,2048]{1,0:T(8,128)(2,1)}, bf16[512,2048]{1,0:T(8,128)(2,1)}, u32[]{:S(2)}, u32[]{:S(2)}) collective-permute-start(bf16[512,2048]{1,0:T(8,128)(2,1)} %constant_dynamic-update-slice_fusion.rest_0_), channel_id=1, source_target_pairs={{0,16},{16,0},{1,17},{17,1},{2,18},{18,2},{3,19},{19,3},{4,20},{20... | collective-permute-start | bytes 6291464 | tf_op jit(solution)/shard_map/ppermute | solution.py:441
  107.9 40.7 %collective-permute-start.10 = (bf16[256,2048]{1,0:T(8,128)(2,1)}, bf16[256,2048]{1,0:T(8,128)(2,1)S(1)}, u32[]{:S(2)}, u32[]{:S(2)}) collective-permute-start(bf16[256,2048]{1,0:T(8,128)(2,1)} %slice.38), channel_id=1, source_target_pairs={{0,32},{32,64},{64,96},{96,0},{1,33},{33,65},{65,97},{97,1},{2,34}... | collective-permute-start | bytes 3145736 | tf_op jit(solution)/shard_map/ppermute | solution.py:421
  111.1 38.3 %collective-permute-start.11 = (bf16[256,2048]{1,0:T(8,128)(2,1)}, bf16[256,2048]{1,0:T(8,128)(2,1)}, u32[]{:S(2)}, u32[]{:S(2)}) collective-permute-start(bf16[256,2048]{1,0:T(8,128)(2,1)} %slice.39), channel_id=1, source_target_pairs={{0,96},{32,0},{64,32},{96,64},{1,97},{33,1},{65,33},{97,65},{2,98}... | collective-permute-start | bytes 3145736 | tf_op jit(solution)/shard_map/ppermute | solution.py:422
  113.2 64.2 %collective-permute-start.13 = (bf16[512,2048]{1,0:T(8,128)(2,1)}, bf16[512,2048]{1,0:T(8,128)(2,1)}, u32[]{:S(2)}, u32[]{:S(2)}) collective-permute-start(bf16[512,2048]{1,0:T(8,128)(2,1)} %collective-permute-done.8.rest_1_), channel_id=1, source_target_pairs={{0,16},{16,0},{1,17},{17,1},{2,18},{18,2},{3,19},{19,3},{4,20},{20... | collective-permute-start | bytes 6291464 | tf_op jit(solution)/shard_map/ppermute | solution.py:441
  124.4 53.0 %collective-permute-start.14 = (bf16[512,2048]{1,0:T(8,128)(2,1)}, bf16[512,2048]{1,0:T(8,128)(2,1)}, u32[]{:S(2)}, u32[]{:S(2)}) collective-permute-start(bf16[512,2048]{1,0:T(8,128)(2,1)} %collective-permute-done.9.rest_2_), channel_id=1, source_target_pairs={{0,16},{16,0},{1,17},{17,1},{2,18},{18,2},{3,19},{19,3},{4,20},{20... | collective-permute-start | bytes 6291464 | tf_op jit(solution)/shard_map/ppermute | solution.py:441
  142.4 35.1 %all-to-all-start.1 = ((bf16[16,256,256]{2,1,0:T(8,128)(2,1)}), bf16[16,256,256]{2,1,0:T(8,128)(2,1)S(1)}, u32[]{:S(2)}, u32[]{:S(2)}) async-start(bf16[16,256,256]{2,1,0:T(8,128)(2,1)} %bitcast.13), calls=%async_computation.1 | async-start | bytes 4194304 | tf_op jit(solution)/shard_map/all_to_all | solution.py:463
  148.5 28.9 %collective-permute-start.15 = (bf16[256,2048]{1,0:T(8,128)(2,1)S(1)}, bf16[256,2048]{1,0:T(8,128)(2,1)}, u32[]{:S(2)}, u32[]{:S(2)}) collective-permute-start(bf16[256,2048]{1,0:T(8,128)(2,1)S(1)} %collective-permute-done.10.rest_3_), channel_id=1, source_target_pairs={{0,16},{16,0},{1,17},{17,1},{2,18},{18,2},{3,19},{19,3},{4,20},{20... | collective-permute-start | bytes 3145736 | tf_op jit(solution)/shard_map/ppermute | solution.py:441
  149.4 28.1 %collective-permute-start.16 = (bf16[256,2048]{1,0:T(8,128)(2,1)}, bf16[256,2048]{1,0:T(8,128)(2,1)}, u32[]{:S(2)}, u32[]{:S(2)}) collective-permute-start(bf16[256,2048]{1,0:T(8,128)(2,1)} %collective-permute-done.11.rest_4_), channel_id=1, source_target_pairs={{0,16},{16,0},{1,17},{17,1},{2,18},{18,2},{3,19},{19,3},{4,20},{20... | collective-permute-start | bytes 3145736 | tf_op jit(solution)/shard_map/ppermute | solution.py:441
  177.5 1.6 copy-start.3
Sparse Core Ops, SparseCore 0:
  10.5 112.8 all-gather.1

commit v4 on v2

--- a/solution.py
+++ b/solution.py
@@ -329,42 +329,56 @@
     )(signal, spec, skip, *table)
 
 
-def project_kernel(queries_ref, mixed_ref, weight_ref, out_ref, gated):
-    parts = mixed_ref.shape[0]
-    width = mixed_ref.shape[2]
-
-    @pl.when(pl.program_id(0) == 0)
-    def _():
-        for j in range(parts):
-            cols = pl.ds(j * width, width)
-            gated[:, cols] = (queries_ref[:, cols].astype(F32) * mixed_ref[j].astype(F32)).astype(BF16)
-
+def gate_kernel(queries_ref, mixed_ref, out_ref):
+    parts, _, width = mixed_ref.shape
+    for j in range(parts):
+        cols = pl.ds(j * width, width)
+        out_ref[:, cols] = (queries_ref[:, cols].astype(F32) * mixed_ref[j].astype(F32)).astype(BF16)
+
+
+def gate(queries, mixed):
+    rows, width = queries.shape
+    parts, _, cols = mixed.shape
+    tile = 64
+    return pl.pallas_call(
+        gate_kernel,
+        grid=(rows // tile,),
+        in_specs=[
+            pl.BlockSpec((tile, width), lambda j: (j, 0)),
+            pl.BlockSpec((parts, tile, cols), lambda j: (0, j, 0)),
+        ],
+        out_specs=pl.BlockSpec((tile, width), lambda j: (j, 0)),
+        out_shape=jax.ShapeDtypeStruct((rows, width), BF16),
+        cost_estimate=pl.CostEstimate(flops=rows * width, bytes_accessed=6 * rows * width, transcendentals=0),
+        name="gate",
+    )(queries, mixed)
+
+
+def project_kernel(gated_ref, weight_ref, out_ref):
     out_ref[...] = lax.dot_general(
-        gated[...], weight_ref[...], (((1,), (1,)), ((), ())), preferred_element_type=F32
+        gated_ref[...], weight_ref[...], (((1,), (1,)), ((), ())), preferred_element_type=F32
     ).astype(BF16)
 
 
-def project(queries, mixed, weight):
-    rows, width = queries.shape
+def project(gated, weight):
+    rows, width = gated.shape
     features = weight.shape[0]
-    tile = 512
+    tile = 1024
     return pl.pallas_call(
         project_kernel,
         grid=(features // tile,),
         in_specs=[
             pl.BlockSpec((rows, width), lambda n: (0, 0)),
-            pl.BlockSpec(mixed.shape, lambda n: (0, 0, 0)),
             pl.BlockSpec((tile, width), lambda n: (n, 0)),
         ],
         out_specs=pl.BlockSpec((rows, tile), lambda n: (0, n)),
         out_shape=jax.ShapeDtypeStruct((rows, features), BF16),
-        scratch_shapes=[pltpu.VMEM((rows, width), BF16)],
-        compiler_params=pltpu.CompilerParams(vmem_limit_bytes=40 * MIB),
+        compiler_params=pltpu.CompilerParams(vmem_limit_bytes=58 * MIB),
         cost_estimate=pl.CostEstimate(
             flops=2 * rows * width * features, bytes_accessed=2 * width * features, transcendentals=0
         ),
         name="project",
-    )(queries, mixed, weight)
+    )(gated, weight)
 
 
 def on_device(queries, keys_in, values_in, filters, skip_gain, out_weight):
@@ -379,7 +393,7 @@
     skip = lax.dynamic_slice_in_dim(skip_gain, lax.axis_index("ctx") * cols, cols).reshape(1, cols)
     mixed = convolve(piece.reshape(count * rows, cols), spec, skip, table)
     returned = lax.all_to_all(mixed.reshape(count, rows, cols), "ctx", split_axis=0, concat_axis=0, tiled=True)
-    return project(queries[0], returned, weight)[None]
+    return project(gate(queries[0], returned), weight)[None]
 
 
 def solution(mesh):

time: 179 us -> 176 us (0.983)
  waiting for transfers between devices: 62.4 us -> 57.5 us
  Pallas kernels: 54.1 us -> 57.4 us
    all_gather x1, waiting for transfers between devices: 54 us -> 49.1 us  [on_device(): weight = lax.all_gather(out_weight.T, ('dp', 'ctx'), axis=0, tiled=True)]
    pallas_call x0 -> x1, Pallas kernels: none -> 4.72 us  [gate(): pl.pallas_call(gate_kernel, grid=(rows // tile,), in_specs=[pl.BlockSpec(...]
    unnamed x8 -> x6, local copies, waits for them, and re-layouts: 8.32 us -> 6.73 us
  transfers between devices with their start and end apart: 2 -> 2, of which waited for: 2 -> 2; matrix products, arithmetic and copies ran while one was open for 0% -> 0% of each run, Pallas kernels for 21% -> 24%
where the time goes in v4:
time: 176 us; the launch traced here: 175 us
  waiting for transfers between devices  57.5 us (33%)
  Pallas kernels  57.4 us (33%)
  blocking collectives  30.8 us (18%)
  between operations  13.4 us (8%)
  starting transfers between devices  8.43 us (5%)
  local copies, waits for them, and re-layouts  7.49 us (4%)
    all_gather x1, waiting for transfers between devices, on_device(): weight = lax.all_gather(out_weight.T, ('dp', 'ctx'), axis=0, tiled=True)  49.1 us
    all_to_all x1, blocking collectives, on_device(): lax.all_to_all(mixed.reshape(count, rows, cols), 'ctx', split_axis=0, con...  30.8 us
    pallas_call x1, Pallas kernels, convolve(): pl.pallas_call(conv_kernel, in_specs=[inside, anywhere, inside] + [anywhe...  16.8 us
    pallas_call x1, Pallas kernels, project(): pl.pallas_call(project_kernel, grid=(features // tile,), in_specs=[pl.Blo...  15.9 us
    pallas_call x1, Pallas kernels, filter_spectrum(): pl.pallas_call(spectrum_kernel, grid=(channels // lanes,), in_specs=[pl.B...  15.7 us
    all_to_all x1, starting transfers between devices, on_device(): lax.all_to_all(product, 'ctx', split_axis=0, concat_axis=0, tiled=True)  8.43 us
    all_to_all x1, waiting for transfers between devices, on_device(): lax.all_to_all(product, 'ctx', split_axis=0, concat_axis=0, tiled=True)  7.68 us
    unnamed x6, local copies, waits for them, and re-layouts  6.73 us
  transfers between devices with their start and end apart: 2, of which 2 were waited for; matrix products, arithmetic and copies ran while one was open for 0% of the time, Pallas kernels for 24%

profile of v4, /device:TPU:1, one launch (start us, length us, event | category | flops | bytes accessed | tf_op | source)
XLA Modules:
  0.0 175.0 jit_solution(3442657569991866956)
XLA Ops:
  6.5 0.0 all-gather.2.cloned.1.call-start
  6.5 0.7 all-gather.2.cloned.1.call-update
  7.3 4.3 %product.1 = bf16[16,256,256]{2,1,0:T(8,128)(2,1)} custom-call(bf16[256,4096]{1,0:T(8,128)(2,1)} %bitcast.11, bf16[256,4096]{1,0:T(8,128)(2,1)} %bitcast.12), custom_call_target="tpu_custom_call" | custom-call | flops 1048576 | bytes 6291456 | tf_op jit(solution)/shard_map/product/pallas_call | solution.py:158
  11.6 8.4 %all-to-all-start = ((bf16[16,256,256]{2,1,0:T(8,128)(2,1)}), bf16[16,256,256]{2,1,0:T(8,128)(2,1)S(1)}, u32[]{:S(2)}, u32[]{:S(2)}) async-start(bf16[16,256,256]{2,1,0:T(8,128)(2,1)} %product.1), calls=%async_computation | async-start | bytes 4194304 | tf_op jit(solution)/shard_map/all_to_all | solution.py:391
  20.0 0.8 dynamic_slice.3
  20.8 0.0 copy-start
  20.8 2.2 %copy-done = bf16[32,256,256]{2,1,0:T(8,128)(2,1)S(1)} copy-done((bf16[32,256,256]{2,1,0:T(8,128)(2,1)S(1)}, bf16[32,256,256]{2,1,0:T(8,128)(2,1)}, u32[]{:S(2)}) %copy-start) | copy-done | bytes 4194328
  23.0 0.0 copy-start.1
  23.0 2.4 %copy-done.1 = bf16[32,256,256]{2,1,0:T(8,128)(2,1)S(1)} copy-done((bf16[32,256,256]{2,1,0:T(8,128)(2,1)S(1)}, bf16[32,256,256]{2,1,0:T(8,128)(2,1)}, u32[]{:S(2)}) %copy-start.1) | copy-done | bytes 4194328
  25.3 0.0 copy-start.2
  25.3 2.2 %copy-done.2 = f32[256,4096]{1,0:T(8,128)S(1)} copy-done((f32[256,4096]{1,0:T(8,128)S(1)}, f32[256,4096]{1,0:T(8,128)}, u32[]{:S(2)}) %copy-start.2) | copy-done | bytes 4194328
  27.5 15.7 %spectrum.1.spec_ref = f32[32,256,256]{2,1,0:T(8,128)} custom-call(f32[256,4096]{1,0:T(8,128)S(1)} %copy-done.2, bf16[32,256,256]{2,1,0:T(8,128)(2,1)S(1)} %copy-done, bf16[32,256,256]{2,1,0:T(8,128)(2,1)S(1)} %copy-done.1), custom_call_target="tpu_custom_call" | custom-call | flops 3221225472 | bytes 33554432 | tf_op jit(solution)/shard_map/spectrum/pallas_call | solution.py:210
  43.2 7.7 %all-to-all-done = bf16[16,256,256]{2,1,0:T(8,128)(2,1)S(1)} async-done(((bf16[16,256,256]{2,1,0:T(8,128)(2,1)}), bf16[16,256,256]{2,1,0:T(8,128)(2,1)S(1)}, u32[]{:S(2)}, u32[]{:S(2)}) %all-to-all-start) | async-done | bytes 2097184 | tf_op jit(solution)/shard_map/all_to_all | solution.py:391
  50.9 16.8 %convolve.1 = bf16[4096,256]{1,0:T(8,128)(2,1)S(1)} custom-call(bf16[4096,256]{1,0:T(8,128)(2,1)S(1)} %bitcast.8, f32[32,256,256]{2,1,0:T(8,128)} %spectrum.1.spec_ref, f32[1,256]{1,0:T(1,128)S(1)} %bitcast.10, bf16[32,256,256]{2,1,0:T(8,128)(2,1)} %constant.18.clone.high_ref.fh_ref, bf16[32,256,256]{2,1,0:T(8,128)(2,1)} %constant.19.clone.low_ref.fl_ref, ...), custom_call_target="tpu_custom_call" | custom-call | flops 6442450944 | bytes 50331648 | tf_op jit(solution)/shard_map/convolve/pallas_call | solution.py:310
  67.7 30.8 %all_to_all.10.mixed_ref = bf16[16,256,256]{2,1,0:T(8,128)(2,1)} all-to-all(bf16[16,256,256]{2,1,0:T(8,128)(2,1)S(1)} %bitcast.9), channel_id=1, replica_groups=mesh['dp'=8,'ctx'=16] {'ctx'}, dimensions={0} | all-to-all | bytes 4194304 | tf_op jit(solution)/shard_map/all_to_all | solution.py:395
  98.4 4.7 %gate.1.gated_ref = bf16[256,4096]{1,0:T(8,128)(2,1)} custom-call(bf16[256,4096]{1,0:T(8,128)(2,1)} %bitcast.13, bf16[16,256,256]{2,1,0:T(8,128)(2,1)} %all_to_all.10.mixed_ref), custom_call_target="tpu_custom_call" | custom-call | flops 1048576 | bytes 6291456 | tf_op jit(solution)/shard_map/gate/pallas_call | solution.py:343
  103.1 49.1 %all-gather.2.cloned.1.call-done.weight_ref = bf16[4096,4096]{1,0:T(8,128)(2,1)} async-done(((bf16[32,4096]{1,0:T(8,128)(2,1)}), bf16[4096,4096]{1,0:T(8,128)(2,1)}) %all-gather.2.cloned.1.call-update) | async-done | bytes 33554448 | tf_op jit(solution)/shard_map/all_gather | solution.py:389
  152.3 15.9 %project.1 = bf16[256,4096]{1,0:T(8,128)(2,1)} custom-call(bf16[256,4096]{1,0:T(8,128)(2,1)} %gate.1.gated_ref, bf16[4096,4096]{1,0:T(8,128)(2,1)} %all-gather.2.cloned.1.call-done.weight_ref), custom_call_target="tpu_custom_call" | custom-call | flops 8589934592 | bytes 33554432 | tf_op jit(solution)/shard_map/project/pallas_call | solution.py:367
Async XLA Ops:
  6.5 145.7 %all-gather.2.cloned.1.call-start = ((), (), s32[]{:S(2)}) async-start(), calls=%async_computation.2 | async-start | bytes 33816576 | tf_op jit(solution)/shard_map/all_gather | solution.py:389
  11.6 39.3 %all-to-all-start = ((bf16[16,256,256]{2,1,0:T(8,128)(2,1)}), bf16[16,256,256]{2,1,0:T(8,128)(2,1)S(1)}, u32[]{:S(2)}, u32[]{:S(2)}) async-start(bf16[16,256,256]{2,1,0:T(8,128)(2,1)} %product.1), calls=%async_computation | async-start | bytes 4194304 | tf_op jit(solution)/shard_map/all_to_all | solution.py:391
  20.8 2.2 %copy-start = (bf16[32,256,256]{2,1,0:T(8,128)(2,1)S(1)}, bf16[32,256,256]{2,1,0:T(8,128)(2,1)}, u32[]{:S(2)}) copy-start(bf16[32,256,256]{2,1,0:T(8,128)(2,1)} %constant.18.clone.high_ref.fh_ref) | copy-start | bytes 12582916
  23.0 2.4 %copy-start.1 = (bf16[32,256,256]{2,1,0:T(8,128)(2,1)S(1)}, bf16[32,256,256]{2,1,0:T(8,128)(2,1)}, u32[]{:S(2)}) copy-start(bf16[32,256,256]{2,1,0:T(8,128)(2,1)} %constant.19.clone.low_ref.fl_ref) | copy-start | bytes 12582916
  25.3 2.2 %copy-start.2 = (f32[256,4096]{1,0:T(8,128)S(1)}, f32[256,4096]{1,0:T(8,128)}, u32[]{:S(2)}) copy-start(f32[256,4096]{1,0:T(8,128)} %filters_ref.1) | copy-start | bytes 12582916
Sparse Core Ops, SparseCore 0:
  10.5 141.7 all-gather.1

commit v5 on v4

--- a/solution.py
+++ b/solution.py
@@ -7,6 +7,7 @@
 from jax import lax
 from jax.experimental import pallas as pl
 from jax.experimental.pallas import tpu as pltpu
+from jax.sharding import Mesh
 from jax.sharding import PartitionSpec as P
 
 F32 = jnp.float32
@@ -354,31 +355,69 @@
     )(queries, mixed)
 
 
-def project_kernel(gated_ref, weight_ref, out_ref):
-    out_ref[...] = lax.dot_general(
+def project_kernel(core_ref, gated_ref, weight_ref, own_ref, other_ref):
+    rows = own_ref.shape[0]
+    result = lax.dot_general(
         gated_ref[...], weight_ref[...], (((1,), (1,)), ((), ())), preferred_element_type=F32
     ).astype(BF16)
-
-
-def project(gated, weight):
-    rows, width = gated.shape
-    features = weight.shape[0]
-    tile = 1024
+    own_ref[...] = result[:rows]
+    other_ref[...] = result[rows:]
+
+
+def project(gated, weight, core):
+    both, width = gated.shape
+    rows = both // 2
+    columns = weight.shape[0]
+    tile = columns // 4
     return pl.pallas_call(
         project_kernel,
-        grid=(features // tile,),
-        in_specs=[
-            pl.BlockSpec((rows, width), lambda n: (0, 0)),
-            pl.BlockSpec((tile, width), lambda n: (n, 0)),
+        grid_spec=pltpu.PrefetchScalarGridSpec(
+            num_scalar_prefetch=1,
+            grid=(4,),
+            in_specs=[
+                pl.BlockSpec((both, width), lambda n, core: (0, 0)),
+                pl.BlockSpec((tile, width), lambda n, core: (n, 0)),
+            ],
+            out_specs=[
+                pl.BlockSpec((rows, tile), lambda n, core: (0, 2 * n + core[0])),
+                pl.BlockSpec((rows, tile), lambda n, core: (0, n)),
+            ],
+        ),
+        out_shape=[
+            jax.ShapeDtypeStruct((rows, 2 * columns), BF16),
+            jax.ShapeDtypeStruct((rows, columns), BF16),
         ],
-        out_specs=pl.BlockSpec((rows, tile), lambda n: (0, n)),
-        out_shape=jax.ShapeDtypeStruct((rows, features), BF16),
         compiler_params=pltpu.CompilerParams(vmem_limit_bytes=58 * MIB),
         cost_estimate=pl.CostEstimate(
-            flops=2 * rows * width * features, bytes_accessed=2 * width * features, transcendentals=0
+            flops=2 * both * width * columns, bytes_accessed=2 * width * columns, transcendentals=0
         ),
         name="project",
-    )(gated, weight)
+    )(core, gated, weight)
+
+
+def fill_kernel(core_ref, part_ref, whole_ref, out_ref):
+    del core_ref, whole_ref
+    out_ref[...] = part_ref[...]
+
+
+def fill(whole, part, core):
+    rows, columns = part.shape
+    tile = columns // 4
+    return pl.pallas_call(
+        fill_kernel,
+        grid_spec=pltpu.PrefetchScalarGridSpec(
+            num_scalar_prefetch=1,
+            grid=(4,),
+            in_specs=[
+                pl.BlockSpec((rows, tile), lambda n, core: (0, n)),
+                pl.BlockSpec(memory_space=pl.ANY),
+            ],
+            out_specs=pl.BlockSpec((rows, tile), lambda n, core: (0, 2 * n + 1 - core[0])),
+        ),
+        out_shape=jax.ShapeDtypeStruct(whole.shape, BF16),
+        input_output_aliases={2: 0},
+        name="fill",
+    )(core, part, whole)
 
 
 def on_device(queries, keys_in, values_in, filters, skip_gain, out_weight):
@@ -386,25 +425,32 @@
     rows, width = queries.shape[1:]
     cols = width // count
     table = [jnp.asarray(t) for t in tables()]
-    weight = lax.all_gather(out_weight.T, ("dp", "ctx"), axis=0, tiled=True)
+    weight = lax.all_gather(out_weight.T, ("y", "ctx"), axis=0, tiled=True)
     product = product_blocks(keys_in[0], values_in[0], count)
     piece = lax.all_to_all(product, "ctx", split_axis=0, concat_axis=0, tiled=True)
     spec = filter_spectrum(filters, table[0], table[1])
     skip = lax.dynamic_slice_in_dim(skip_gain, lax.axis_index("ctx") * cols, cols).reshape(1, cols)
     mixed = convolve(piece.reshape(count * rows, cols), spec, skip, table)
     returned = lax.all_to_all(mixed.reshape(count, rows, cols), "ctx", split_axis=0, concat_axis=0, tiled=True)
-    return project(gate(queries[0], returned), weight)[None]
+    cores = [(0, 1), (1, 0)]
+    own = gate(queries[0], returned)
+    other = lax.ppermute(own, "core", cores)
+    core = lax.axis_index("core").astype(jnp.int32).reshape(1)
+    whole, apart = project(jnp.concatenate([own, other], axis=0), weight, core)
+    return fill(whole, lax.ppermute(apart, "core", cores), core)[None]
 
 
 def solution(mesh):
+    chips = Mesh(mesh.devices.reshape(4, 2, 16), ("y", "core", "ctx"))
+    dp = ("y", "core")
     in_specs = (
-        P("dp", "ctx", None),
-        P("dp", "ctx", None),
-        P("dp", "ctx", None),
+        P(dp, "ctx", None),
+        P(dp, "ctx", None),
+        P(dp, "ctx", None),
         P("ctx", None),
         P(),
-        P(None, ("dp", "ctx")),
+        P(None, dp + ("ctx",)),
     )
     return jax.shard_map(
-        on_device, mesh=mesh, in_specs=in_specs, out_specs=P("dp", "ctx", None), check_vma=False
+        on_device, mesh=chips, in_specs=in_specs, out_specs=P(dp, "ctx", None), check_vma=False
     )

time: 176 us -> 175 us (level)
  waiting for transfers between devices: 57.5 us -> 47.6 us
  other arithmetic: 0 us -> 4.04 us
  starting transfers between devices: 8.43 us -> 12 us
    all_gather x1, waiting for transfers between devices: 49.1 us -> 32.6 us  [on_device(): weight = lax.all_gather(out_weight.T, ('y', 'ctx'), axis=0, tiled=True)]
    ppermute x0 -> x2, waiting for transfers between devices: none -> 6.49 us  [the longest x1 4 us: on_device(): other = lax.ppermute(own, 'core', cores)]
    concatenate x0 -> x1, other arithmetic: none -> 4.04 us  [on_device(): whole, apart = project(jnp.concatenate([own, other], axis=0), weight, core)]
    ppermute x0 -> x2, starting transfers between devices: none -> 3.55 us  [the longest x1 2.97 us: on_device(): other = lax.ppermute(own, 'core', cores)]
    pallas_call x1 -> x2, Pallas kernels: 15.9 us -> 17.1 us  [the longest x1 13.8 us: project(): pl.pallas_call(project_kernel, grid_spec=pltpu.PrefetchScalarGridSpec(num...]
    unnamed x6 -> x8, local copies, waits for them, and re-layouts: 6.73 us -> 7.68 us
  transfers between devices with their start and end apart: 2 -> 4, of which waited for: 2 -> 4; matrix products, arithmetic and copies ran while one was open for 0% -> 3% of each run, Pallas kernels for 24% -> 24%
where the time goes in v5:
time: 175 us; the launch traced here: 174 us
  Pallas kernels  58.2 us (33%)
  waiting for transfers between devices  47.6 us (27%)
  blocking collectives  30.6 us (17%)
  between operations  13.4 us (8%)
  starting transfers between devices  12 us (7%)
  local copies, waits for them, and re-layouts  8.45 us (5%)
  other arithmetic  4.04 us (2%)
    all_gather x1, waiting for transfers between devices, on_device(): weight = lax.all_gather(out_weight.T, ('y', 'ctx'), axis=0, tiled=True)  32.6 us
    all_to_all x1, blocking collectives, on_device(): lax.all_to_all(mixed.reshape(count, rows, cols), 'ctx', split_axis=0, con...  30.6 us
    pallas_call x1, Pallas kernels, convolve(): pl.pallas_call(conv_kernel, in_specs=[inside, anywhere, inside] + [anywhe...  16.8 us
    pallas_call x1, Pallas kernels, filter_spectrum(): pl.pallas_call(spectrum_kernel, grid=(channels // lanes,), in_specs=[pl.B...  15.7 us
    pallas_call x1, Pallas kernels, project(): pl.pallas_call(project_kernel, grid_spec=pltpu.PrefetchScalarGridSpec(num...  13.8 us
    all_to_all x1, starting transfers between devices, on_device(): lax.all_to_all(product, 'ctx', split_axis=0, concat_axis=0, tiled=True)  8.43 us
    all_to_all x1, waiting for transfers between devices, on_device(): lax.all_to_all(product, 'ctx', split_axis=0, concat_axis=0, tiled=True)  7.74 us
    unnamed x8, local copies, waits for them, and re-layouts  7.68 us
  transfers between devices with their start and end apart: 4, of which 4 were waited for; matrix products, arithmetic and copies ran while one was open for 3% of the time, Pallas kernels for 24%

profile of v5, /device:TPU:1, one launch (start us, length us, event | category | flops | bytes accessed | tf_op | source)
XLA Modules:
  0.0 174.3 jit_solution(2140308325579292663)
XLA Ops:
  6.5 0.0 all-gather.2.cloned.1.call-start
  6.5 0.7 all-gather.2.cloned.1.call-update
  7.3 4.3 %product.1 = bf16[16,256,256]{2,1,0:T(8,128)(2,1)} custom-call(bf16[256,4096]{1,0:T(8,128)(2,1)} %bitcast.12, bf16[256,4096]{1,0:T(8,128)(2,1)} %bitcast.13), custom_call_target="tpu_custom_call" | custom-call | flops 1048576 | bytes 6291456 | tf_op jit(solution)/shard_map/product/pallas_call | solution.py:159
  11.6 8.4 %all-to-all-start = ((bf16[16,256,256]{2,1,0:T(8,128)(2,1)}), bf16[16,256,256]{2,1,0:T(8,128)(2,1)S(1)}, u32[]{:S(2)}, u32[]{:S(2)}) async-start(bf16[16,256,256]{2,1,0:T(8,128)(2,1)} %product.1), calls=%async_computation | async-start | bytes 4194304 | tf_op jit(solution)/shard_map/all_to_all | solution.py:430
  20.0 0.8 dynamic_slice.3
  20.8 0.0 copy-start
  20.8 2.2 %copy-done = bf16[32,256,256]{2,1,0:T(8,128)(2,1)S(1)} copy-done((bf16[32,256,256]{2,1,0:T(8,128)(2,1)S(1)}, bf16[32,256,256]{2,1,0:T(8,128)(2,1)}, u32[]{:S(2)}) %copy-start) | copy-done | bytes 4194328
  23.0 0.0 copy-start.1
  23.0 2.3 %copy-done.1 = bf16[32,256,256]{2,1,0:T(8,128)(2,1)S(1)} copy-done((bf16[32,256,256]{2,1,0:T(8,128)(2,1)S(1)}, bf16[32,256,256]{2,1,0:T(8,128)(2,1)}, u32[]{:S(2)}) %copy-start.1) | copy-done | bytes 4194328
  25.3 2.2 %copy-done.2 = f32[256,4096]{1,0:T(8,128)S(1)} copy-done((f32[256,4096]{1,0:T(8,128)S(1)}, f32[256,4096]{1,0:T(8,128)}, u32[]{:S(2)}) %copy-start.2) | copy-done | bytes 4194328
  27.5 15.7 %spectrum.1.spec_ref = f32[32,256,256]{2,1,0:T(8,128)} custom-call(f32[256,4096]{1,0:T(8,128)S(1)} %copy-done.2, bf16[32,256,256]{2,1,0:T(8,128)(2,1)S(1)} %copy-done, bf16[32,256,256]{2,1,0:T(8,128)(2,1)S(1)} %copy-done.1), custom_call_target="tpu_custom_call" | custom-call | flops 3221225472 | bytes 33554432 | tf_op jit(solution)/shard_map/spectrum/pallas_call | solution.py:211
  43.2 7.7 %all-to-all-done = bf16[16,256,256]{2,1,0:T(8,128)(2,1)S(1)} async-done(((bf16[16,256,256]{2,1,0:T(8,128)(2,1)}), bf16[16,256,256]{2,1,0:T(8,128)(2,1)S(1)}, u32[]{:S(2)}, u32[]{:S(2)}) %all-to-all-start) | async-done | bytes 2097184 | tf_op jit(solution)/shard_map/all_to_all | solution.py:430
  50.9 16.8 %convolve.1 = bf16[4096,256]{1,0:T(8,128)(2,1)S(1)} custom-call(bf16[4096,256]{1,0:T(8,128)(2,1)S(1)} %bitcast.9, f32[32,256,256]{2,1,0:T(8,128)} %spectrum.1.spec_ref, f32[1,256]{1,0:T(1,128)S(1)} %bitcast.11, bf16[32,256,256]{2,1,0:T(8,128)(2,1)} %constant.23.clone.high_ref.fh_ref, bf16[32,256,256]{2,1,0:T(8,128)(2,1)} %constant.24.clone.low_ref.fl_ref, ...), custom_call_target="tpu_custom_call" | custom-call | flops 6442450944 | bytes 50331648 | tf_op jit(solution)/shard_map/convolve/pallas_call | solution.py:311
  67.7 30.6 %all_to_all.10.mixed_ref = bf16[16,256,256]{2,1,0:T(8,128)(2,1)} all-to-all(bf16[16,256,256]{2,1,0:T(8,128)(2,1)S(1)} %bitcast.10), channel_id=1, replica_groups=mesh['y'=4,'core'=2,'ctx'=16] {'ctx'}, dimensions={0} | all-to-all | bytes 4194304 | tf_op jit(solution)/shard_map/all_to_all | solution.py:434
  98.3 4.3 %gate.1 = bf16[256,4096]{1,0:T(8,128)(2,1)} custom-call(bf16[256,4096]{1,0:T(8,128)(2,1)} %bitcast.14, bf16[16,256,256]{2,1,0:T(8,128)(2,1)} %all_to_all.10.mixed_ref), custom_call_target="tpu_custom_call" | custom-call | flops 1048576 | bytes 6291456 | tf_op jit(solution)/shard_map/gate/pallas_call | solution.py:344
  102.6 3.0 %collective-permute-start = (bf16[256,4096]{1,0:T(8,128)(2,1)}, bf16[256,4096]{1,0:T(8,128)(2,1)S(1)}, u32[]{:S(2)}, u32[]{:S(2)}) collective-permute-start(bf16[256,4096]{1,0:T(8,128)(2,1)} %gate.1), channel_id=1, source_target_pairs={{0,16},{16,0},{1,17},{17,1},{2,18},{18,2},{3,19},{19,3},{4,20},{20... | collective-permute-start | bytes 6291464 | tf_op jit(solution)/shard_map/ppermute | solution.py:437
  105.6 4.0 %collective-permute-done = bf16[256,4096]{1,0:T(8,128)(2,1)S(1)} collective-permute-done((bf16[256,4096]{1,0:T(8,128)(2,1)}, bf16[256,4096]{1,0:T(8,128)(2,1)S(1)}, u32[]{:S(2)}, u32[]{:S(2)}) %collective-permute-start) | collective-permute-done | bytes 2097184 | tf_op jit(solution)/shard_map/ppermute | solution.py:437
  109.6 4.0 %pad_maximum_fusion.gated_ref = bf16[512,4096]{1,0:T(8,128)(2,1)} fusion(bf16[256,4096]{1,0:T(8,128)(2,1)S(1)} %collective-permute-done, bf16[256,4096]{1,0:T(8,128)(2,1)} %gate.1), kind=kLoop, calls=%fused_computation | loop fusion | flops 8388608 | bytes 8388608 | tf_op jit(solution)/shard_map/concatenate | solution.py:439
  113.6 32.6 %all-gather.2.cloned.1.call-done.weight_ref = bf16[2048,4096]{1,0:T(8,128)(2,1)} async-done(((bf16[32,4096]{1,0:T(8,128)(2,1)}), bf16[2048,4096]{1,0:T(8,128)(2,1)}) %all-gather.2.cloned.1.call-update) | async-done | bytes 16777232 | tf_op jit(solution)/shard_map/all_gather | solution.py:428
  146.3 13.8 %project.1 = (bf16[256,4096]{1,0:T(8,128)(2,1)}, bf16[256,2048]{1,0:T(8,128)(2,1)}) custom-call(s32[1]{0:T(128)} %bitcast.core_ref, bf16[512,4096]{1,0:T(8,128)(2,1)} %pad_maximum_fusion.gated_ref, bf16[2048,4096]{1,0:T(8,128)(2,1)} %all-gather.2.cloned.1.call-done.weight_ref), custom_call_target="tpu_custom_call" | custom-call | flops 8589934592 | bytes 16777216 | tf_op jit(solution)/shard_map/project/pallas_call | solution.py:372
  160.0 0.6 collective-permute-start.1
  160.6 2.5 %collective-permute-done.1.part_ref = bf16[256,2048]{1,0:T(8,128)(2,1)S(1)} collective-permute-done((bf16[256,2048]{1,0:T(8,128)(2,1)}, bf16[256,2048]{1,0:T(8,128)(2,1)S(1)}, u32[]{:S(2)}, u32[]{:S(2)}) %collective-permute-start.1) | collective-permute-done | bytes 1048608 | tf_op jit(solution)/shard_map/ppermute | solution.py:440
  163.1 1.0 copy-done.3
  164.1 3.4 %fill.1 = bf16[256,4096]{1,0:T(8,128)(2,1)} custom-call(s32[1]{0:T(128)} %bitcast.core_ref, bf16[256,2048]{1,0:T(8,128)(2,1)} %copy-done.3, bf16[256,4096]{1,0:T(8,128)(2,1)} %get-tuple-element.8.whole_ref), custom_call_target="tpu_custom_call", output_to_operand_aliasing={{}: (2, {})} | custom-call | tf_op jit(solution)/shard_map/fill/pallas_call | solution.py:406
  (2 shorter events, 0.0 us)
Async XLA Ops:
  6.5 139.7 %all-gather.2.cloned.1.call-start = ((), (), s32[]{:S(2)}) async-start(), calls=%async_computation.2 | async-start | bytes 17039360 | tf_op jit(solution)/shard_map/all_gather | solution.py:428
  11.6 39.3 %all-to-all-start = ((bf16[16,256,256]{2,1,0:T(8,128)(2,1)}), bf16[16,256,256]{2,1,0:T(8,128)(2,1)S(1)}, u32[]{:S(2)}, u32[]{:S(2)}) async-start(bf16[16,256,256]{2,1,0:T(8,128)(2,1)} %product.1), calls=%async_computation | async-start | bytes 4194304 | tf_op jit(solution)/shard_map/all_to_all | solution.py:430
  20.8 2.2 %copy-start = (bf16[32,256,256]{2,1,0:T(8,128)(2,1)S(1)}, bf16[32,256,256]{2,1,0:T(8,128)(2,1)}, u32[]{:S(2)}) copy-start(bf16[32,256,256]{2,1,0:T(8,128)(2,1)} %constant.23.clone.high_ref.fh_ref) | copy-start | bytes 12582916
  23.0 2.3 %copy-start.1 = (bf16[32,256,256]{2,1,0:T(8,128)(2,1)S(1)}, bf16[32,256,256]{2,1,0:T(8,128)(2,1)}, u32[]{:S(2)}) copy-start(bf16[32,256,256]{2,1,0:T(8,128)(2,1)} %constant.24.clone.low_ref.fl_ref) | copy-start | bytes 12582916
  25.3 2.2 %copy-start.2 = (f32[256,4096]{1,0:T(8,128)S(1)}, f32[256,4096]{1,0:T(8,128)}, u32[]{:S(2)}) copy-start(f32[256,4096]{1,0:T(8,128)} %filters_ref.1) | copy-start | bytes 12582916
  102.6 7.0 %collective-permute-start = (bf16[256,4096]{1,0:T(8,128)(2,1)}, bf16[256,4096]{1,0:T(8,128)(2,1)S(1)}, u32[]{:S(2)}, u32[]{:S(2)}) collective-permute-start(bf16[256,4096]{1,0:T(8,128)(2,1)} %gate.1), channel_id=1, source_target_pairs={{0,16},{16,0},{1,17},{17,1},{2,18},{18,2},{3,19},{19,3},{4,20},{20... | collective-permute-start | bytes 6291464 | tf_op jit(solution)/shard_map/ppermute | solution.py:437
  160.0 3.1 %collective-permute-start.1 = (bf16[256,2048]{1,0:T(8,128)(2,1)}, bf16[256,2048]{1,0:T(8,128)(2,1)S(1)}, u32[]{:S(2)}, u32[]{:S(2)}) collective-permute-start(bf16[256,2048]{1,0:T(8,128)(2,1)} %get-tuple-element.7), channel_id=1, source_target_pairs={{0,16},{16,0},{1,17},{17,1},{2,18},{18,2},{3,19},{19,3},{4,20},{20... | collective-permute-start | bytes 3145736 | tf_op jit(solution)/shard_map/ppermute | solution.py:440
  163.1 1.0 copy-start.3
Sparse Core Ops, SparseCore 0:
  10.2 135.9 all-gather.1

commit v6 on v5

--- a/solution.py
+++ b/solution.py
@@ -395,27 +395,31 @@
     )(core, gated, weight)
 
 
-def fill_kernel(core_ref, part_ref, whole_ref, out_ref):
-    del core_ref, whole_ref
-    out_ref[...] = part_ref[...]
+def fill_kernel(core_ref, part_ref, whole_ref, out_ref, sems):
+    del whole_ref
+    tile = part_ref.shape[1] // 4
+    copies = []
+    for n in range(4):
+        start = pl.multiple_of((2 * n + 1 - core_ref[0]) * tile, tile)
+        copies.append(
+            pltpu.make_async_copy(part_ref.at[:, pl.ds(n * tile, tile)], out_ref.at[:, pl.ds(start, tile)], sems.at[n])
+        )
+    for copy in copies:
+        copy.start()
+    for copy in copies:
+        copy.wait()
 
 
 def fill(whole, part, core):
-    rows, columns = part.shape
-    tile = columns // 4
+    anywhere = pl.BlockSpec(memory_space=pl.ANY)
     return pl.pallas_call(
         fill_kernel,
-        grid_spec=pltpu.PrefetchScalarGridSpec(
-            num_scalar_prefetch=1,
-            grid=(4,),
-            in_specs=[
-                pl.BlockSpec((rows, tile), lambda n, core: (0, n)),
-                pl.BlockSpec(memory_space=pl.ANY),
-            ],
-            out_specs=pl.BlockSpec((rows, tile), lambda n, core: (0, 2 * n + 1 - core[0])),
-        ),
+        in_specs=[pl.BlockSpec(memory_space=pltpu.SMEM), anywhere, anywhere],
+        out_specs=anywhere,
         out_shape=jax.ShapeDtypeStruct(whole.shape, BF16),
+        scratch_shapes=[pltpu.SemaphoreType.DMA((4,))],
         input_output_aliases={2: 0},
+        compiler_params=pltpu.CompilerParams(vmem_limit_bytes=58 * MIB),
         name="fill",
     )(core, part, whole)
 

time: 175 us -> 204 us (1.17)
  Pallas kernels: 58.2 us -> 87.7 us
    pallas_call x1, Pallas kernels: 3.36 us -> 32.9 us  [fill(): pl.pallas_call(fill_kernel, in_specs=[pl.BlockSpec(memory_space=pltpu.SME...]
  transfers between devices with their start and end apart: 4 -> 4, of which waited for: 4 -> 4; matrix products, arithmetic and copies ran while one was open for 3% -> 2% of each run, Pallas kernels for 24% -> 20%
where the time goes in v6:
time: 204 us
  Pallas kernels  87.7 us (43%)
  waiting for transfers between devices  47.6 us (23%)
  blocking collectives  30.6 us (15%)
  between operations  13.4 us (7%)
  starting transfers between devices  12 us (6%)
  local copies, waits for them, and re-layouts  8.45 us (4%)
  other arithmetic  4.04 us (2%)
    pallas_call x1, Pallas kernels, fill(): pl.pallas_call(fill_kernel, in_specs=[pl.BlockSpec(memory_space=pltpu.SME...  32.9 us
    all_gather x1, waiting for transfers between devices, on_device(): weight = lax.all_gather(out_weight.T, ('y', 'ctx'), axis=0, tiled=True)  32.6 us
    all_to_all x1, blocking collectives, on_device(): lax.all_to_all(mixed.reshape(count, rows, cols), 'ctx', split_axis=0, con...  30.6 us
    pallas_call x1, Pallas kernels, convolve(): pl.pallas_call(conv_kernel, in_specs=[inside, anywhere, inside] + [anywhe...  16.8 us
    pallas_call x1, Pallas kernels, filter_spectrum(): pl.pallas_call(spectrum_kernel, grid=(channels // lanes,), in_specs=[pl.B...  15.7 us
    pallas_call x1, Pallas kernels, project(): pl.pallas_call(project_kernel, grid_spec=pltpu.PrefetchScalarGridSpec(num...  13.8 us
    all_to_all x1, starting transfers between devices, on_device(): lax.all_to_all(product, 'ctx', split_axis=0, concat_axis=0, tiled=True)  8.43 us
    all_to_all x1, waiting for transfers between devices, on_device(): lax.all_to_all(product, 'ctx', split_axis=0, concat_axis=0, tiled=True)  7.74 us
  transfers between devices with their start and end apart: 4, of which 4 were waited for; matrix products, arithmetic and copies ran while one was open for 2% of the time, Pallas kernels for 20%

profile of v6, /device:TPU:1, one launch (start us, length us, event | category | flops | bytes accessed | tf_op | source)
XLA Modules:
  0.0 203.8 jit_solution(4671463221320482137)
XLA Ops:
  6.5 0.0 all-gather.2.cloned.1.call-start
  6.5 0.7 all-gather.2.cloned.1.call-update
  7.3 4.3 %product.1 = bf16[16,256,256]{2,1,0:T(8,128)(2,1)} custom-call(bf16[256,4096]{1,0:T(8,128)(2,1)} %bitcast.12, bf16[256,4096]{1,0:T(8,128)(2,1)} %bitcast.13), custom_call_target="tpu_custom_call" | custom-call | flops 1048576 | bytes 6291456 | tf_op jit(solution)/shard_map/product/pallas_call | solution.py:159
  11.6 8.4 %all-to-all-start = ((bf16[16,256,256]{2,1,0:T(8,128)(2,1)}), bf16[16,256,256]{2,1,0:T(8,128)(2,1)S(1)}, u32[]{:S(2)}, u32[]{:S(2)}) async-start(bf16[16,256,256]{2,1,0:T(8,128)(2,1)} %product.1), calls=%async_computation | async-start | bytes 4194304 | tf_op jit(solution)/shard_map/all_to_all | solution.py:434
  20.0 0.8 dynamic_slice.3
  20.8 0.0 copy-start
  20.8 2.2 %copy-done = bf16[32,256,256]{2,1,0:T(8,128)(2,1)S(1)} copy-done((bf16[32,256,256]{2,1,0:T(8,128)(2,1)S(1)}, bf16[32,256,256]{2,1,0:T(8,128)(2,1)}, u32[]{:S(2)}) %copy-start) | copy-done | bytes 4194328
  23.0 0.0 copy-start.1
  23.0 2.3 %copy-done.1 = bf16[32,256,256]{2,1,0:T(8,128)(2,1)S(1)} copy-done((bf16[32,256,256]{2,1,0:T(8,128)(2,1)S(1)}, bf16[32,256,256]{2,1,0:T(8,128)(2,1)}, u32[]{:S(2)}) %copy-start.1) | copy-done | bytes 4194328
  25.3 2.2 %copy-done.2 = f32[256,4096]{1,0:T(8,128)S(1)} copy-done((f32[256,4096]{1,0:T(8,128)S(1)}, f32[256,4096]{1,0:T(8,128)}, u32[]{:S(2)}) %copy-start.2) | copy-done | bytes 4194328
  27.5 15.7 %spectrum.1.spec_ref = f32[32,256,256]{2,1,0:T(8,128)} custom-call(f32[256,4096]{1,0:T(8,128)S(1)} %copy-done.2, bf16[32,256,256]{2,1,0:T(8,128)(2,1)S(1)} %copy-done, bf16[32,256,256]{2,1,0:T(8,128)(2,1)S(1)} %copy-done.1), custom_call_target="tpu_custom_call" | custom-call | flops 3221225472 | bytes 33554432 | tf_op jit(solution)/shard_map/spectrum/pallas_call | solution.py:211
  43.2 7.7 %all-to-all-done = bf16[16,256,256]{2,1,0:T(8,128)(2,1)S(1)} async-done(((bf16[16,256,256]{2,1,0:T(8,128)(2,1)}), bf16[16,256,256]{2,1,0:T(8,128)(2,1)S(1)}, u32[]{:S(2)}, u32[]{:S(2)}) %all-to-all-start) | async-done | bytes 2097184 | tf_op jit(solution)/shard_map/all_to_all | solution.py:434
  50.9 16.8 %convolve.1 = bf16[4096,256]{1,0:T(8,128)(2,1)S(1)} custom-call(bf16[4096,256]{1,0:T(8,128)(2,1)S(1)} %bitcast.9, f32[32,256,256]{2,1,0:T(8,128)} %spectrum.1.spec_ref, f32[1,256]{1,0:T(1,128)S(1)} %bitcast.11, bf16[32,256,256]{2,1,0:T(8,128)(2,1)} %constant.23.clone.high_ref.fh_ref, bf16[32,256,256]{2,1,0:T(8,128)(2,1)} %constant.24.clone.low_ref.fl_ref, ...), custom_call_target="tpu_custom_call" | custom-call | flops 6442450944 | bytes 50331648 | tf_op jit(solution)/shard_map/convolve/pallas_call | solution.py:311
  67.7 30.6 %all_to_all.10.mixed_ref = bf16[16,256,256]{2,1,0:T(8,128)(2,1)} all-to-all(bf16[16,256,256]{2,1,0:T(8,128)(2,1)S(1)} %bitcast.10), channel_id=1, replica_groups=mesh['y'=4,'core'=2,'ctx'=16] {'ctx'}, dimensions={0} | all-to-all | bytes 4194304 | tf_op jit(solution)/shard_map/all_to_all | solution.py:438
  98.3 4.3 %gate.1 = bf16[256,4096]{1,0:T(8,128)(2,1)} custom-call(bf16[256,4096]{1,0:T(8,128)(2,1)} %bitcast.14, bf16[16,256,256]{2,1,0:T(8,128)(2,1)} %all_to_all.10.mixed_ref), custom_call_target="tpu_custom_call" | custom-call | flops 1048576 | bytes 6291456 | tf_op jit(solution)/shard_map/gate/pallas_call | solution.py:344
  102.6 3.0 %collective-permute-start = (bf16[256,4096]{1,0:T(8,128)(2,1)}, bf16[256,4096]{1,0:T(8,128)(2,1)S(1)}, u32[]{:S(2)}, u32[]{:S(2)}) collective-permute-start(bf16[256,4096]{1,0:T(8,128)(2,1)} %gate.1), channel_id=1, source_target_pairs={{0,16},{16,0},{1,17},{17,1},{2,18},{18,2},{3,19},{19,3},{4,20},{20... | collective-permute-start | bytes 6291464 | tf_op jit(solution)/shard_map/ppermute | solution.py:441
  105.6 4.0 %collective-permute-done = bf16[256,4096]{1,0:T(8,128)(2,1)S(1)} collective-permute-done((bf16[256,4096]{1,0:T(8,128)(2,1)}, bf16[256,4096]{1,0:T(8,128)(2,1)S(1)}, u32[]{:S(2)}, u32[]{:S(2)}) %collective-permute-start) | collective-permute-done | bytes 2097184 | tf_op jit(solution)/shard_map/ppermute | solution.py:441
  109.6 4.0 %pad_maximum_fusion.gated_ref = bf16[512,4096]{1,0:T(8,128)(2,1)} fusion(bf16[256,4096]{1,0:T(8,128)(2,1)S(1)} %collective-permute-done, bf16[256,4096]{1,0:T(8,128)(2,1)} %gate.1), kind=kLoop, calls=%fused_computation | loop fusion | flops 8388608 | bytes 8388608 | tf_op jit(solution)/shard_map/concatenate | solution.py:443
  113.6 32.6 %all-gather.2.cloned.1.call-done.weight_ref = bf16[2048,4096]{1,0:T(8,128)(2,1)} async-done(((bf16[32,4096]{1,0:T(8,128)(2,1)}), bf16[2048,4096]{1,0:T(8,128)(2,1)}) %all-gather.2.cloned.1.call-update) | async-done | bytes 16777232 | tf_op jit(solution)/shard_map/all_gather | solution.py:432
  146.3 13.8 %project.1 = (bf16[256,4096]{1,0:T(8,128)(2,1)}, bf16[256,2048]{1,0:T(8,128)(2,1)}) custom-call(s32[1]{0:T(128)} %bitcast.core_ref, bf16[512,4096]{1,0:T(8,128)(2,1)} %pad_maximum_fusion.gated_ref, bf16[2048,4096]{1,0:T(8,128)(2,1)} %all-gather.2.cloned.1.call-done.weight_ref), custom_call_target="tpu_custom_call" | custom-call | flops 8589934592 | bytes 16777216 | tf_op jit(solution)/shard_map/project/pallas_call | solution.py:372
  160.0 0.6 collective-permute-start.1
  160.6 2.5 %collective-permute-done.1.part_ref = bf16[256,2048]{1,0:T(8,128)(2,1)S(1)} collective-permute-done((bf16[256,2048]{1,0:T(8,128)(2,1)}, bf16[256,2048]{1,0:T(8,128)(2,1)S(1)}, u32[]{:S(2)}, u32[]{:S(2)}) %collective-permute-start.1) | collective-permute-done | bytes 1048608 | tf_op jit(solution)/shard_map/ppermute | solution.py:444
  163.1 1.0 copy-done.3
  164.1 32.9 %fill.1 = bf16[256,4096]{1,0:T(8,128)(2,1)} custom-call(s32[1]{0:T(128)} %bitcast.core_ref, bf16[256,2048]{1,0:T(8,128)(2,1)} %copy-done.3, bf16[256,4096]{1,0:T(8,128)(2,1)} %get-tuple-element.8.whole_ref), custom_call_target="tpu_custom_call", output_to_operand_aliasing={{}: (2, {})} | custom-call | tf_op jit(solution)/shard_map/fill/pallas_call | solution.py:415
  (2 shorter events, 0.0 us)
Async XLA Ops:
  6.5 139.7 %all-gather.2.cloned.1.call-start = ((), (), s32[]{:S(2)}) async-start(), calls=%async_computation.2 | async-start | bytes 17039360 | tf_op jit(solution)/shard_map/all_gather | solution.py:432
  11.6 39.3 %all-to-all-start = ((bf16[16,256,256]{2,1,0:T(8,128)(2,1)}), bf16[16,256,256]{2,1,0:T(8,128)(2,1)S(1)}, u32[]{:S(2)}, u32[]{:S(2)}) async-start(bf16[16,256,256]{2,1,0:T(8,128)(2,1)} %product.1), calls=%async_computation | async-start | bytes 4194304 | tf_op jit(solution)/shard_map/all_to_all | solution.py:434
  20.8 2.2 %copy-start = (bf16[32,256,256]{2,1,0:T(8,128)(2,1)S(1)}, bf16[32,256,256]{2,1,0:T(8,128)(2,1)}, u32[]{:S(2)}) copy-start(bf16[32,256,256]{2,1,0:T(8,128)(2,1)} %constant.23.clone.high_ref.fh_ref) | copy-start | bytes 12582916
  23.0 2.3 %copy-start.1 = (bf16[32,256,256]{2,1,0:T(8,128)(2,1)S(1)}, bf16[32,256,256]{2,1,0:T(8,128)(2,1)}, u32[]{:S(2)}) copy-start(bf16[32,256,256]{2,1,0:T(8,128)(2,1)} %constant.24.clone.low_ref.fl_ref) | copy-start | bytes 12582916
  25.3 2.2 %copy-start.2 = (f32[256,4096]{1,0:T(8,128)S(1)}, f32[256,4096]{1,0:T(8,128)}, u32[]{:S(2)}) copy-start(f32[256,4096]{1,0:T(8,128)} %filters_ref.1) | copy-start | bytes 12582916
  102.6 7.0 %collective-permute-start = (bf16[256,4096]{1,0:T(8,128)(2,1)}, bf16[256,4096]{1,0:T(8,128)(2,1)S(1)}, u32[]{:S(2)}, u32[]{:S(2)}) collective-permute-start(bf16[256,4096]{1,0:T(8,128)(2,1)} %gate.1), channel_id=1, source_target_pairs={{0,16},{16,0},{1,17},{17,1},{2,18},{18,2},{3,19},{19,3},{4,20},{20... | collective-permute-start | bytes 6291464 | tf_op jit(solution)/shard_map/ppermute | solution.py:441
  160.0 3.1 %collective-permute-start.1 = (bf16[256,2048]{1,0:T(8,128)(2,1)}, bf16[256,2048]{1,0:T(8,128)(2,1)S(1)}, u32[]{:S(2)}, u32[]{:S(2)}) collective-permute-start(bf16[256,2048]{1,0:T(8,128)(2,1)} %get-tuple-element.7), channel_id=1, source_target_pairs={{0,16},{16,0},{1,17},{17,1},{2,18},{18,2},{3,19},{19,3},{4,20},{20... | collective-permute-start | bytes 3145736 | tf_op jit(solution)/shard_map/ppermute | solution.py:444
  163.1 1.0 copy-start.3
Sparse Core Ops, SparseCore 0:
  10.2 135.9 all-gather.1
